TPU v7x, 32 devices: a whole 2x2x4 slice. The times are simulated.
32 devices in a mesh: section: 4 (over y, x), fsdp: 8 (over z, core).
Axes of the slice: x: 2, y: 2, z: 4, core: 2. Of those that a mesh axis runs over, the one named last changes fastest.
Arguments:
- section_inputs: bfloat16 [4, 2, 1024, 8192], P('section', None, 'fsdp'), may hold values from -6 to 6
- top_grads: bfloat16 [2, 1024, 8192], P(None, 'fsdp'), may hold values from -6 to 6
- weights: bfloat16 [4, 8192, 512], P('section', 'fsdp'), may hold values from -0.125 to 0.125
- norm_gains: float32 [4, 8192], P('section', 'fsdp'), may hold values from 0.25 to 1.75
- feedback: float32 [4, 1024, 8192], P('section', 'fsdp'), may hold values from -4 to 4
- rotation_bits: int32 [4, 8192], replicated, may hold values from 0 to 1
- batch_order: int32 [2], replicated, may hold values from 0 to 1, each once
Outputs:
- input_grads: float32 [4, 2, 1024, 8192], P('section', None, 'fsdp')
- weight_grads: float32 [4, 8192, 512], P('section', 'fsdp')
- gain_grads: float32 [4, 8192], P('section', 'fsdp')
- feedback_out: float32 [4, 1024, 8192], P('section', 'fsdp')
Inputs may be any that keep to these rules, and one draw needn't show every extreme that they name: `batch_order`: a permutation of the micro-batches.
All inputs are finite; a program needn't handle non-finite values.
Results may differ from a plain program's by a relative error of at most 0.035.
Values may be sent and summed in bfloat16 or wider, within the bound.
A program may use at most 192 MiB of HBM per device.

v0:
```python
import jax
import jax.numpy as jnp
from jax import lax
from jax.sharding import PartitionSpec as P

HB = 256


eps_norm = 1e-05
eps_scale = 1e-06
highest = lax.Precision.HIGHEST


def shifted(value, axis, by):
    length = lax.axis_size(axis)
    pairs = [(i, i + by) for i in range(length) if 0 <= i + by < length]
    return lax.ppermute(value, axis, pairs)


def hadamard(order_size):
    position = jnp.arange(order_size, dtype=jnp.int32)
    shared_bits = jnp.bitwise_and(position[:, None], position[None, :])
    parity = jnp.zeros((order_size, order_size), jnp.int32)
    for bit_place in range(order_size.bit_length() - 1):
        parity = parity + jnp.bitwise_and(jnp.right_shift(shared_bits, bit_place), 1)
    return (1 - 2 * (parity % 2)).astype(jnp.float32) / jnp.sqrt(jnp.float32(order_size))


def rotate(values, sign_row, matrix):
    block_size = matrix.shape[0]
    blocks = (values * sign_row).reshape(values.shape[0], values.shape[1] // block_size, block_size)
    return jnp.einsum("tbk,kj->tbj", blocks, matrix, precision=highest)


def restore(rotated, sign_row, matrix):
    unrotated = jnp.einsum("tbk,kj->tbj", rotated, matrix, precision=highest)
    return unrotated.reshape(unrotated.shape[0], -1) * sign_row


def layer_backward(inputs, grad_in, gain_row, weight):
    token_count = inputs.shape[0]
    values = inputs.astype(jnp.float32)
    scale_inv = lax.rsqrt(jnp.mean(values * values, axis=-1, keepdims=True) + eps_norm)
    normed = values * scale_inv
    hidden_in = (normed * gain_row).astype(jnp.bfloat16)
    grad_low = grad_in.astype(jnp.bfloat16)
    joined = jnp.dot(
        jnp.concatenate([hidden_in, grad_low], axis=0), weight, preferred_element_type=jnp.float32
    )
    pre = joined[:token_count]
    grad_act = joined[token_count:]
    sigma = jax.nn.sigmoid(pre)
    active_out = (pre * sigma).astype(jnp.bfloat16)
    grad_pre = (grad_act * sigma * (1.0 + pre * (1.0 - sigma))).astype(jnp.bfloat16)
    grad_hidden = lax.dot_general(
        grad_pre, weight, (((1,), (1,)), ((), ())), preferred_element_type=jnp.float32
    )
    gain_term = jnp.sum(grad_hidden * normed, axis=0)
    grad_normed = grad_hidden * gain_row
    grad_out = grad_in + scale_inv * (
        grad_normed - normed * jnp.mean(grad_normed * normed, axis=-1, keepdims=True)
    )
    return (grad_out, gain_term, hidden_in, grad_low, grad_pre, active_out)


def per_device(
    section_inputs, top_grads, weights, norm_gains, feedback, rotation_bits, batch_order
):
    section_count = lax.axis_size("section")
    section_here = lax.axis_index("section")
    micro_count = section_inputs.shape[1]
    token_count = section_inputs.shape[2]
    feature_count = section_inputs.shape[3]
    adapter = weights.shape[2]
    block_count = feature_count // HB
    weight = lax.all_gather(weights[0], "fsdp", axis=0, tiled=True)
    gain_row = lax.all_gather(norm_gains[0], "fsdp", axis=0, tiled=True)
    matrix = hadamard(HB)
    sign_rows = (1 - 2 * rotation_bits).astype(jnp.float32)
    own_signs = lax.dynamic_index_in_dim(sign_rows, section_here, 0, keepdims=False)
    above_signs = lax.dynamic_index_in_dim(
        sign_rows, jnp.minimum(section_here + 1, section_count - 1), 0, keepdims=False
    )
    local_inputs = section_inputs[0]
    is_last = section_here == section_count - 1

    def tick_step(tick, state):
        (
            in_levels,
            in_scales,
            carried,
            kept_hidden,
            kept_grad,
            kept_pre,
            kept_act,
            grads_kept,
            gain_sum,
        ) = state
        slot = tick - (section_count - 1 - section_here)
        live = jnp.logical_and(slot >= 0, slot < micro_count)
        micro = lax.dynamic_index_in_dim(
            batch_order, jnp.clip(slot, 0, micro_count - 1), 0, keepdims=False
        )
        from_top = lax.dynamic_index_in_dim(top_grads, micro, 0, keepdims=False).astype(jnp.float32)
        arrived = (
            in_levels.reshape(token_count, block_count, HB).astype(jnp.float32)
            * in_scales.astype(jnp.float32)[..., None]
        )
        from_below = restore(arrived, above_signs, matrix)
        grad_in = jnp.where(is_last, from_top, from_below)

        def work(operands):
            carried_w, hidden_w, grad_w, pre_w, act_w, out_w, gain_w = operands
            inputs = lax.dynamic_index_in_dim(local_inputs, micro, 0, keepdims=False)
            grad_out, gain_term, hidden_in, grad_low, grad_pre, active_out = layer_backward(
                inputs, grad_in, gain_row, weight
            )
            total = grad_out + carried_w
            rotated = rotate(total, own_signs, matrix)
            scale_low = (jnp.mean(jnp.abs(rotated), axis=-1) + eps_scale).astype(jnp.bfloat16)
            scale_wide = scale_low.astype(jnp.float32)[..., None]
            levels = jnp.clip(rotated / scale_wide, -1.0, 1.0).astype(jnp.bfloat16)
            decoded = restore(levels.astype(jnp.float32) * scale_wide, own_signs, matrix)
            new_carried = jnp.where(section_here > 0, total - decoded, carried_w)
            return (
                levels.reshape(token_count, feature_count),
                scale_low,
                new_carried,
                lax.dynamic_update_index_in_dim(hidden_w, hidden_in, micro, 0),
                lax.dynamic_update_index_in_dim(grad_w, grad_low, micro, 0),
                lax.dynamic_update_index_in_dim(pre_w, grad_pre, micro, 0),
                lax.dynamic_update_index_in_dim(act_w, active_out, micro, 0),
                lax.dynamic_update_index_in_dim(out_w, grad_out, micro, 0),
                gain_w + gain_term,
            )

        def skip(operands):
            carried_w, hidden_w, grad_w, pre_w, act_w, out_w, gain_w = operands
            return (
                jnp.zeros((token_count, feature_count), jnp.bfloat16),
                jnp.zeros((token_count, block_count), jnp.bfloat16),
                carried_w,
                hidden_w,
                grad_w,
                pre_w,
                act_w,
                out_w,
                gain_w,
            )

        results = lax.cond(
            live,
            work,
            skip,
            (carried, kept_hidden, kept_grad, kept_pre, kept_act, grads_kept, gain_sum),
        )
        sent_levels, sent_scales = shifted((results[0], results[1]), "section", -1)
        return (sent_levels, sent_scales) + tuple(results[2:])

    start_state = (
        jnp.zeros((token_count, feature_count), jnp.bfloat16),
        jnp.zeros((token_count, block_count), jnp.bfloat16),
        feedback[0],
        jnp.zeros((micro_count, token_count, feature_count), jnp.bfloat16),
        jnp.zeros((micro_count, token_count, feature_count), jnp.bfloat16),
        jnp.zeros((micro_count, token_count, adapter), jnp.bfloat16),
        jnp.zeros((micro_count, token_count, adapter), jnp.bfloat16),
        jnp.zeros((micro_count, token_count, feature_count), jnp.float32),
        jnp.zeros((feature_count,), jnp.float32),
    )
    final_state = lax.fori_loop(0, section_count + micro_count - 1, tick_step, start_state)
    (
        last_levels,
        last_scales,
        carried,
        kept_hidden,
        kept_grad,
        kept_pre,
        kept_act,
        grads_kept,
        gain_sum,
    ) = final_state
    gain_share = lax.psum_scatter(gain_sum, "fsdp", scatter_dimension=0, tiled=True)
    stacked_in = jnp.concatenate(
        [kept_hidden.reshape(-1, feature_count), kept_grad.reshape(-1, feature_count)], axis=0
    )
    stacked_out = jnp.concatenate(
        [kept_pre.reshape(-1, adapter), kept_act.reshape(-1, adapter)], axis=0
    )
    weight_share = lax.psum_scatter(
        lax.dot_general(
            stacked_in, stacked_out, (((0,), (0,)), ((), ())), preferred_element_type=jnp.float32
        ),
        "fsdp",
        scatter_dimension=0,
        tiled=True,
    )
    return (grads_kept[None], weight_share[None], gain_share[None], carried[None])


def solution(mesh):
    return jax.shard_map(
        per_device,
        mesh=mesh,
        in_specs=(
            P("section", None, "fsdp", None),
            P(None, "fsdp", None),
            P("section", "fsdp", None),
            P("section", "fsdp"),
            P("section", "fsdp", None),
            P(),
            P(),
        ),
        out_specs=(
            P("section", None, "fsdp", None),
            P("section", "fsdp", None),
            P("section", "fsdp"),
            P("section", "fsdp", None),
        ),
        check_vma=False,
    )
```

profile of v0, /device:TPU:0, one launch (start us, length us, event | category | flops | bytes accessed | tf_op | source)
XLA Modules:
  0.0 971.5 jit_solution(15982574916865978980)
XLA Ops:
  7.2 4.6 copy.94
  12.0 15.7 %all-gather = f32[1,8192]{1,0:T(1,128)S(1)} all-gather(f32[1,1024]{1,0:T(1,128)S(1)} %copy-done.3), channel_id=2, replica_groups=mesh['section'=4,'fsdp'=8] {'fsdp'}, dimensions={1}, use_global_device_ids=true | all-gather | bytes 36864 | tf_op jit(solution)/shard_map/all_gather | solution.py:77
  27.8 69.0 %all-gather.4.cloned.1.call-done = bf16[1,8192,512]{2,1,0:T(8,128)(2,1)} async-done(((bf16[1,1024,512]{2,1,0:T(8,128)(2,1)}), bf16[1,8192,512]{2,1,0:T(8,128)(2,1)}) %all-gather.4.cloned.1.call-update) | async-done | bytes 8388624 | tf_op jit(solution)/shard_map/all_gather | solution.py:76
  96.8 4.4 broadcast_in_dim.54
  101.2 2.4 broadcast.120
  103.6 2.4 broadcast.120.clone
  106.4 678.5 %while.32 = (s32[]{:T(128)}, bf16[128,8192]{0,1:T(8,128)(2,1)S(1)}, bf16[128,32]{0,1:T(8,128)(2,1)S(1)}, f32[128,8192]{1,0:T(8,128)}, bf16[2,128,8192]{2,1,0:T(8...) while((s32[]{:T(128)}, bf16[128,8192]{0,1:T(8,128)(2,1)S(1)}, ...), condition=%wide.region_7.8_spmd.clone.clone, body=%wide.region_0.7_spmd.clone.clone.sunk | while | flops 12950519808 | bytes 267181360 | solution.py:171
  107.0 3.4 copy.39
  110.4 7.9 fusion.75
  118.4 1.6 conditional.4
  118.4 1.6 broadcast.105
  121.2 1.3 collective-permute-start.1
  122.6 47.5 %collective-permute-done.1 = bf16[128,32]{0,1:T(8,128)(2,1)S(1)} collective-permute-done((bf16[128,32]{0,1:T(8,128)(2,1)S(1)}, bf16[128,32]{0,1:T(8,128)(2,1)S(1)}, u32[]{:S(2)}, u32[]{:S(2)}) %collective-permute-start.1) | collective-permute-done | bytes 8224 | tf_op jit(solution)/shard_map/while/body/eval_jaxpr/ppermute | solution.py:17
  170.4 3.4 copy.39
  173.8 7.9 fusion.75
  181.7 1.6 conditional.4
  181.7 1.6 broadcast.105
  185.9 47.3 %collective-permute-done.1 = bf16[128,32]{0,1:T(8,128)(2,1)S(1)} collective-permute-done((bf16[128,32]{0,1:T(8,128)(2,1)S(1)}, bf16[128,32]{0,1:T(8,128)(2,1)S(1)}, u32[]{:S(2)}, u32[]{:S(2)}) %collective-permute-start.1) | collective-permute-done | bytes 8224 | tf_op jit(solution)/shard_map/while/body/eval_jaxpr/ppermute | solution.py:17
  233.5 3.4 copy.39
  236.9 7.9 fusion.75
  244.9 1.6 conditional.4
  244.9 1.6 broadcast.105
  249.0 262.3 %collective-permute-done.1 = bf16[128,32]{0,1:T(8,128)(2,1)S(1)} collective-permute-done((bf16[128,32]{0,1:T(8,128)(2,1)S(1)}, bf16[128,32]{0,1:T(8,128)(2,1)S(1)}, u32[]{:S(2)}, u32[]{:S(2)}) %collective-permute-start.1) | collective-permute-done | bytes 8224 | tf_op jit(solution)/shard_map/while/body/eval_jaxpr/ppermute | solution.py:17
  511.6 3.4 copy.39
  515.1 7.9 fusion.75
  523.0 75.3 %conditional.4 = (bf16[128,8192]{0,1:T(8,128)(2,1)}, bf16[128,32]{0,1:T(8,128)(2,1)S(1)}, f32[128,8192]{1,0:T(8,128)}, bf16[2,128,8192]{2,1,0:T(8,128)(2,1)}, bf...) conditional(s32[]{:T(128)} %convert_element_type.222, ...), branch_computations={%region_1.1_spmd, %region_2.6_spmd} | conditional | flops 9723129856 | bytes 243776256 | solution.py:151
  525.5 2.1 fusion.16
  527.6 2.8 copy.28
  533.5 2.2 copy-done.4
  535.7 2.3 fusion.22
  538.2 4.8 fusion.15
  543.0 6.4 bitcast_dynamic-update-slice_fusion
  549.4 4.7 broadcast_multiply_fusion
  554.1 3.8 abs_reduce_fusion
  558.8 5.7 fusion.26
  564.5 5.2 copy.29
  569.7 7.6 subtract_select_fusion
  577.3 2.8 copy.21
  580.2 6.6 copy.24
  586.8 4.9 reshape.115
  591.7 6.6 fusion.29
  600.9 45.7 %collective-permute-done.1 = bf16[128,32]{0,1:T(8,128)(2,1)S(1)} collective-permute-done((bf16[128,32]{0,1:T(8,128)(2,1)S(1)}, bf16[128,32]{0,1:T(8,128)(2,1)S(1)}, u32[]{:S(2)}, u32[]{:S(2)}) %collective-permute-start.1) | collective-permute-done | bytes 8224 | tf_op jit(solution)/shard_map/while/body/eval_jaxpr/ppermute | solution.py:17
  647.0 3.4 copy.39
  650.4 7.9 fusion.75
  658.3 75.3 %conditional.4 = (bf16[128,8192]{0,1:T(8,128)(2,1)}, bf16[128,32]{0,1:T(8,128)(2,1)S(1)}, f32[128,8192]{1,0:T(8,128)}, bf16[2,128,8192]{2,1,0:T(8,128)(2,1)}, bf...) conditional(s32[]{:T(128)} %convert_element_type.222, ...), branch_computations={%region_1.1_spmd, %region_2.6_spmd} | conditional | flops 9723129856 | bytes 243776256 | solution.py:151
  660.8 2.1 fusion.16
  662.9 2.8 copy.28
  668.8 2.2 copy-done.4
  671.0 2.3 fusion.22
  673.5 4.8 fusion.15
  678.3 6.4 bitcast_dynamic-update-slice_fusion
  684.7 4.7 broadcast_multiply_fusion
  689.5 3.8 abs_reduce_fusion
  694.2 5.7 fusion.26
  699.8 5.2 copy.29
  705.1 7.6 subtract_select_fusion
  712.7 2.8 copy.21
  715.5 6.6 copy.24
  722.1 4.9 reshape.115
  727.0 6.6 fusion.29
  736.2 44.8 %collective-permute-done.1 = bf16[128,32]{0,1:T(8,128)(2,1)S(1)} collective-permute-done((bf16[128,32]{0,1:T(8,128)(2,1)S(1)}, bf16[128,32]{0,1:T(8,128)(2,1)S(1)}, u32[]{:S(2)}, u32[]{:S(2)}) %collective-permute-start.1) | collective-permute-done | bytes 8224 | tf_op jit(solution)/shard_map/while/body/eval_jaxpr/ppermute | solution.py:17
  785.0 13.8 %fusion.55 = f32[8192,512]{1,0:T(8,128)} fusion(bf16[256,8192]{1,0:T(8,128)(2,1)} %bitcast.17, bf16[256,8192]{1,0:T(8,128)(2,1)} %bitcast.16, bf16[256,512]{1,0:T(8,128)(2,1)S(1)} %bitcast.103, bf16[256,512]{1,0:T(8,128)(2,1)S(1)} %bitcast.102), kind=kOutput, calls=%fused_computation.74 | convolution fusion | flops 4312793088 | bytes 25690112 | tf_op jit(solution)/shard_map/dot_general | solution.py:191
  800.6 27.1 %all-reduce = f32[8192]{0:T(1024)S(1)} all-reduce(f32[8192]{0:T(1024)S(1)} %get-tuple-element.650), channel_id=5, replica_groups=mesh['section'=4,'fsdp'=8] {'fsdp'}, use_global_device_ids=true, to_apply=%region_9.10.clone | all-reduce | flops 8192 | bytes 65536
  828.4 136.1 %reduce-scatter.2.cloned.1.call-done = f32[1024,512]{1,0:T(8,128)} async-done(((f32[8192,512]{1,0:T(8,128)}), f32[1024,512]{1,0:T(8,128)}) %reduce-scatter.2.cloned.1.call-update) | async-done | bytes 2097168 | tf_op jit(solution)/shard_map/reduce_scatter | solution.py:190
  (74 shorter events, 25.1 us)
Async XLA Ops:
  7.2 4.8 copy-start.3
  7.2 20.5 %copy-start.2 = (s32[4,8192]{1,0:T(4,128)S(1)}, s32[4,8192]{1,0:T(4,128)}, u32[]{:S(2)}) copy-start(s32[4,8192]{1,0:T(4,128)} %param.16) | copy-start | bytes 393220
  7.2 89.6 %all-gather.4.cloned.1.call-start = ((), (), s32[]{:S(2)}) async-start(), calls=%async_computation.2 | async-start | bytes 9437184 | tf_op jit(solution)/shard_map/all_gather | solution.py:76
  11.9 952.6 %reduce-scatter.2.cloned.1.call-start = ((), (), s32[]{:S(2)}) async-start(), calls=%async_computation.1 | async-start | bytes 18874368 | tf_op jit(solution)/shard_map/reduce_scatter | solution.py:190
  103.6 2.8 copy-start.5
  120.0 50.1 %collective-permute-start = (bf16[128,8192]{0,1:T(8,128)(2,1)}, bf16[128,8192]{0,1:T(8,128)(2,1)S(1)}, u32[]{:S(2)}, u32[]{:S(2)}) collective-permute-start(bf16[128,8192]{0,1:T(8,128)(2,1)} %get-tuple-element.1011), channel_id=1, source_target_pairs={{8,0},{16,8},{24,16},{9,1},{17,9},{25,17},{10,2},{18,10},{26,18},{... | collective-permute-start | bytes 6291464 | tf_op jit(solution)/shard_map/while/body/eval_jaxpr/ppermute | solution.py:17
  121.2 48.8 %collective-permute-start.1 = (bf16[128,32]{0,1:T(8,128)(2,1)S(1)}, bf16[128,32]{0,1:T(8,128)(2,1)S(1)}, u32[]{:S(2)}, u32[]{:S(2)}) collective-permute-start(bf16[128,32]{0,1:T(8,128)(2,1)S(1)} %get-tuple-element.1012), channel_id=1, source_target_pairs={{8,0},{16,8},{24,16},{9,1},{17,9},{25,17},{10,2},{18,10},{26,18},{... | collective-permute-start | bytes 24584 | tf_op jit(solution)/shard_map/while/body/eval_jaxpr/ppermute | solution.py:17
  183.3 49.9 %collective-permute-start = (bf16[128,8192]{0,1:T(8,128)(2,1)}, bf16[128,8192]{0,1:T(8,128)(2,1)S(1)}, u32[]{:S(2)}, u32[]{:S(2)}) collective-permute-start(bf16[128,8192]{0,1:T(8,128)(2,1)} %get-tuple-element.1011), channel_id=1, source_target_pairs={{8,0},{16,8},{24,16},{9,1},{17,9},{25,17},{10,2},{18,10},{26,18},{... | collective-permute-start | bytes 6291464 | tf_op jit(solution)/shard_map/while/body/eval_jaxpr/ppermute | solution.py:17
  184.6 48.6 %collective-permute-start.1 = (bf16[128,32]{0,1:T(8,128)(2,1)S(1)}, bf16[128,32]{0,1:T(8,128)(2,1)S(1)}, u32[]{:S(2)}, u32[]{:S(2)}) collective-permute-start(bf16[128,32]{0,1:T(8,128)(2,1)S(1)} %get-tuple-element.1012), channel_id=1, source_target_pairs={{8,0},{16,8},{24,16},{9,1},{17,9},{25,17},{10,2},{18,10},{26,18},{... | collective-permute-start | bytes 24584 | tf_op jit(solution)/shard_map/while/body/eval_jaxpr/ppermute | solution.py:17
  246.5 264.8 %collective-permute-start = (bf16[128,8192]{0,1:T(8,128)(2,1)}, bf16[128,8192]{0,1:T(8,128)(2,1)S(1)}, u32[]{:S(2)}, u32[]{:S(2)}) collective-permute-start(bf16[128,8192]{0,1:T(8,128)(2,1)} %get-tuple-element.1011), channel_id=1, source_target_pairs={{8,0},{16,8},{24,16},{9,1},{17,9},{25,17},{10,2},{18,10},{26,18},{... | collective-permute-start | bytes 6291464 | tf_op jit(solution)/shard_map/while/body/eval_jaxpr/ppermute | solution.py:17
  247.7 263.6 %collective-permute-start.1 = (bf16[128,32]{0,1:T(8,128)(2,1)S(1)}, bf16[128,32]{0,1:T(8,128)(2,1)S(1)}, u32[]{:S(2)}, u32[]{:S(2)}) collective-permute-start(bf16[128,32]{0,1:T(8,128)(2,1)S(1)} %get-tuple-element.1012), channel_id=1, source_target_pairs={{8,0},{16,8},{24,16},{9,1},{17,9},{25,17},{10,2},{18,10},{26,18},{... | collective-permute-start | bytes 24584 | tf_op jit(solution)/shard_map/while/body/eval_jaxpr/ppermute | solution.py:17
  527.6 3.5 copy-start
  527.6 4.7 copy-start.1
  532.3 3.4 copy-start.4
  598.3 48.3 %collective-permute-start = (bf16[128,8192]{0,1:T(8,128)(2,1)}, bf16[128,8192]{0,1:T(8,128)(2,1)S(1)}, u32[]{:S(2)}, u32[]{:S(2)}) collective-permute-start(bf16[128,8192]{0,1:T(8,128)(2,1)} %get-tuple-element.1011), channel_id=1, source_target_pairs={{8,0},{16,8},{24,16},{9,1},{17,9},{25,17},{10,2},{18,10},{26,18},{... | collective-permute-start | bytes 6291464 | tf_op jit(solution)/shard_map/while/body/eval_jaxpr/ppermute | solution.py:17
  599.6 47.0 %collective-permute-start.1 = (bf16[128,32]{0,1:T(8,128)(2,1)S(1)}, bf16[128,32]{0,1:T(8,128)(2,1)S(1)}, u32[]{:S(2)}, u32[]{:S(2)}) collective-permute-start(bf16[128,32]{0,1:T(8,128)(2,1)S(1)} %get-tuple-element.1012), channel_id=1, source_target_pairs={{8,0},{16,8},{24,16},{9,1},{17,9},{25,17},{10,2},{18,10},{26,18},{... | collective-permute-start | bytes 24584 | tf_op jit(solution)/shard_map/while/body/eval_jaxpr/ppermute | solution.py:17
  662.9 3.5 copy-start
  662.9 4.7 copy-start.1
  667.7 3.4 copy-start.4
  733.6 47.4 %collective-permute-start = (bf16[128,8192]{0,1:T(8,128)(2,1)}, bf16[128,8192]{0,1:T(8,128)(2,1)S(1)}, u32[]{:S(2)}, u32[]{:S(2)}) collective-permute-start(bf16[128,8192]{0,1:T(8,128)(2,1)} %get-tuple-element.1011), channel_id=1, source_target_pairs={{8,0},{16,8},{24,16},{9,1},{17,9},{25,17},{10,2},{18,10},{26,18},{... | collective-permute-start | bytes 6291464 | tf_op jit(solution)/shard_map/while/body/eval_jaxpr/ppermute | solution.py:17
  734.9 46.1 %collective-permute-start.1 = (bf16[128,32]{0,1:T(8,128)(2,1)S(1)}, bf16[128,32]{0,1:T(8,128)(2,1)S(1)}, u32[]{:S(2)}, u32[]{:S(2)}) collective-permute-start(bf16[128,32]{0,1:T(8,128)(2,1)S(1)} %get-tuple-element.1012), channel_id=1, source_target_pairs={{8,0},{16,8},{24,16},{9,1},{17,9},{25,17},{10,2},{18,10},{26,18},{... | collective-permute-start | bytes 24584 | tf_op jit(solution)/shard_map/while/body/eval_jaxpr/ppermute | solution.py:17
  798.7 0.7 copy-start.6
Sparse Core Ops, SparseCore 0:
  12.0 84.7 all-gather.3
  798.9 165.5 reduce-scatter.1
where the time goes:
time: 984 us; the launch traced here: 972 us
  waiting for transfers between devices  653 us (66%)
  local copies, waits for them, and re-layouts  92.1 us (9%)
  matrix products  86.6 us (9%)
  other arithmetic  61 us (6%)
  blocking collectives  42.8 us (4%)
  between operations  15 us (2%)
  starting transfers between devices  12.9 us (1%)
    ppermute x10, waiting for transfers between devices, shifted(): return lax.ppermute(value, axis, pairs)  448 us
    reduce_scatter x1, waiting for transfers between devices, per_device(): lax.psum_scatter(lax.dot_general(stacked_in, stacked_out, (((0,), (0,)),...  136 us
    all_gather x1, waiting for transfers between devices, per_device(): weight = lax.all_gather(weights[0], 'fsdp', axis=0, tiled=True)  69 us
    dot_general x7, matrix products, restore(): unrotated = jnp.einsum('tbk,kj->tbj', rotated, matrix, precision=highest)  50.9 us
    unnamed x1, blocking collectives  27.1 us
    another operation x14, local copies, waits for them, and re-layouts  23.1 us
  transfers between devices with their start and end apart: 12, of which 7 were waited for; matrix products, arithmetic and copies ran while one was open for 0% of the time, Pallas kernels for 0%

commit v1 on v0

v1 whole, which is shorter than its diff:
```python
import functools

import jax
import jax.numpy as jnp
from jax import lax
from jax.experimental import pallas as pl
from jax.experimental.pallas import tpu as pltpu
from jax.sharding import PartitionSpec as P

HB = 256
CHUNK = 32
SLOTS = 4
LANES = 128
GROUP = 4
MESH = pl.DeviceIdType.MESH

eps_norm = 1e-05
eps_scale = 1e-06
f32 = jnp.float32
bf16 = jnp.bfloat16


def hadamard(order_size):
    position = jnp.arange(order_size, dtype=jnp.int32)
    shared_bits = jnp.bitwise_and(position[:, None], position[None, :])
    parity = jnp.zeros((order_size, order_size), jnp.int32)
    for bit_place in range(order_size.bit_length() - 1):
        parity = parity + jnp.bitwise_and(jnp.right_shift(shared_bits, bit_place), 1)
    return (1 - 2 * (parity % 2)).astype(f32) / jnp.sqrt(f32(order_size))


def dot(a, b, ca=1, cb=0):
    return lax.dot_general(a, b, (((ca,), (cb,)), ((), ())), preferred_element_type=f32)


def relay_kernel(
    sections, x, top, weight, gain, signs, matrix, fb_in,
    gout, dw, gsum, fb,
    inbox, outbox, hidden, stage, pre, gp, act, sinv, gacc,
    recv_sem, send_sem, out_sem, fb_sem, top_sem,
):
    sec = lax.axis_index("section")
    rows_all, width = x.shape
    rank = weight.shape[1]
    held = fb.shape[0]
    chunks = rows_all // CHUNK
    last = sections - 1
    barrier = pltpu.get_barrier_semaphore()

    @pl.when(sec < last)
    def _():
        pl.semaphore_signal(barrier, inc=1, device_id={"section": sec + 1}, device_id_type=MESH)

    fb_copy = pltpu.make_async_copy(fb_in, fb, fb_sem)
    fb_copy.start()
    top_copy = pltpu.make_async_copy(top, inbox.at[:, pl.ds(0, width)], top_sem)

    @pl.when(sec == last)
    def _():
        top_copy.start()

    gacc[...] = jnp.zeros_like(gacc)
    wide = 1024

    @pl.loop(0, chunks)
    def _(c):
        rows = pl.ds(pl.multiple_of(c * CHUNK, CHUNK), CHUNK)

        def square(k, acc):
            part = x[rows, pl.ds(pl.multiple_of(k * wide, wide), wide)].astype(f32)
            part = part * part
            for j in range(wide // LANES):
                acc = acc + part[:, j * LANES:(j + 1) * LANES]
            return acc

        acc = lax.fori_loop(0, width // wide, square, jnp.zeros((CHUNK, LANES), f32))
        scale_inv = lax.rsqrt(jnp.sum(acc, axis=-1, keepdims=True) / width + eps_norm)
        sinv[rows, :] = jnp.broadcast_to(scale_inv, (CHUNK, LANES))

        @pl.loop(0, width // wide)
        def _(k):
            cols = pl.ds(pl.multiple_of(k * wide, wide), wide)
            hidden[rows, cols] = (x[rows, cols].astype(f32) * scale_inv * gain[:, cols]).astype(bf16)

    pre[...] = jnp.zeros_like(pre)

    @pl.loop(0, width // wide)
    def _(k):
        cols = pl.ds(pl.multiple_of(k * wide, wide), wide)
        pre[...] += dot(hidden[:, cols], weight[cols, :])

    fb_copy.wait()

    @pl.when(sec == last)
    def _():
        top_copy.wait()

    @pl.when(sec > 0)
    def _():
        pl.semaphore_wait(barrier, 1)

    lane = lax.broadcasted_iota(jnp.int32, (CHUNK, LANES), 1)
    group_wide = GROUP * HB

    def send(c, slot):
        return pltpu.make_async_remote_copy(
            src_ref=outbox.at[slot],
            dst_ref=inbox.at[pl.ds(pl.multiple_of(c * CHUNK, CHUNK), CHUNK)],
            send_sem=send_sem.at[slot],
            recv_sem=recv_sem.at[c],
            device_id={"section": sec - 1},
            device_id_type=MESH,
        )

    def store(c, half):
        return pltpu.make_async_copy(
            stage.at[half],
            gout.at[pl.ds(pl.multiple_of(c * CHUNK, CHUNK), CHUNK)],
            out_sem.at[half],
        )

    @pl.loop(0, chunks)
    def _(c):
        rows = pl.ds(pl.multiple_of(c * CHUNK, CHUNK), CHUNK)
        kept = pl.ds(pl.multiple_of(lax.rem(c * CHUNK, held), CHUNK), CHUNK)
        half = lax.rem(c, 2)
        slot = lax.rem(c, SLOTS)

        @pl.when(c >= 2)
        def _():
            store(c - 2, half).wait()

        @pl.when(sec == last)
        def _():
            @pl.loop(0, width // wide)
            def _(k):
                cols = pl.ds(pl.multiple_of(k * wide, wide), wide)
                stage[half, :, cols] = inbox[rows, cols].astype(f32)

        @pl.when(sec < last)
        def _():
            send(c, slot).wait_recv()
            scales = inbox[rows, pl.ds(width, LANES)].astype(f32)

            @pl.loop(0, width // group_wide)
            def _(k):
                for j in range(GROUP):
                    block = k * GROUP + j
                    cols = pl.ds(pl.multiple_of(block * HB, HB), HB)
                    scale = jnp.sum(jnp.where(lane == block, scales, 0.0), axis=-1, keepdims=True)
                    value = dot(inbox[rows, cols], matrix[...]) * scale * signs[1:2, cols]
                    stage[half, :, cols] = value
                    inbox[rows, cols] = value.astype(bf16)

        def multiply(k, acc):
            cols = pl.ds(pl.multiple_of(k * wide, wide), wide)
            return acc + dot(inbox[rows, cols], weight[cols, :])

        grad_act = lax.fori_loop(0, width // wide, multiply, jnp.zeros((CHUNK, rank), f32))
        pre_here = pre[rows, :]
        sigma = jax.nn.sigmoid(pre_here)
        act[rows, :] = (pre_here * sigma).astype(bf16)
        grad_pre = (grad_act * sigma * (1.0 + pre_here * (1.0 - sigma))).astype(bf16)
        gp[rows, :] = grad_pre
        inner = jnp.sum(grad_pre.astype(f32) * pre_here, axis=-1, keepdims=True) / width
        scale_inv = sinv[rows, 0:1]

        def layer_block(cols):
            grad_hidden = dot(grad_pre, weight[cols, :], 1, 1)
            normed = x[rows, cols].astype(f32) * scale_inv
            term = grad_hidden * normed
            total = term[0:8]
            for j in range(1, CHUNK // 8):
                total = total + term[8 * j:8 * j + 8]
            gacc[:, cols] += total
            grad_out = stage[half, :, cols] + scale_inv * (grad_hidden * gain[:, cols] - normed * inner)
            stage[half, :, cols] = grad_out
            return grad_out

        @pl.when(sec == 0)
        def _():
            @pl.loop(0, width // group_wide)
            def _(k):
                for j in range(GROUP):
                    layer_block(pl.ds(pl.multiple_of((k * GROUP + j) * HB, HB), HB))

        @pl.when(sec > 0)
        def _():
            @pl.when(c >= SLOTS)
            def _():
                send(c - SLOTS, slot).wait_send()

            def encode(k, scales):
                for j in range(GROUP):
                    block = k * GROUP + j
                    cols = pl.ds(pl.multiple_of(block * HB, HB), HB)
                    value = layer_block(cols) + fb[kept, cols]
                    sign = signs[0:1, cols]
                    turned = value * sign
                    high = turned.astype(bf16)
                    low = (turned - high.astype(f32)).astype(bf16)
                    rotated = dot(high, matrix[...]) + dot(low, matrix[...])
                    scale = jnp.sum(jnp.abs(rotated), axis=-1, keepdims=True) / HB + eps_scale
                    scale = scale.astype(bf16).astype(f32)
                    levels = jnp.clip(rotated * (1.0 / scale), -1.0, 1.0).astype(bf16)
                    outbox[slot, :, cols] = levels
                    fb[kept, cols] = value - dot(levels, matrix[...]) * scale * sign
                    scales = jnp.where(lane == block, scale, scales)
                return scales

            scales = lax.fori_loop(0, width // group_wide, encode, jnp.zeros((CHUNK, LANES), f32))
            outbox[slot, :, pl.ds(width, LANES)] = scales.astype(bf16)
            send(c, slot).start()

        store(c, half).start()

    @pl.loop(0, width // HB)
    def _(k):
        cols = pl.ds(pl.multiple_of(k * HB, HB), HB)
        dw[cols, :] = (dot(hidden[:, cols], gp[...], 0, 0) + dot(inbox[:, pl.ds(pl.multiple_of(k * HB, HB), HB)], act[...], 0, 0)).astype(dw.dtype)

    gsum[...] = jnp.sum(gacc[...], axis=0, keepdims=True)
    for c in range(max(0, chunks - 2), chunks):
        store(c, c % 2).wait()

    @pl.when(sec > 0)
    def _():
        for c in range(max(0, chunks - SLOTS), chunks):
            send(c, c % SLOTS).wait_send()


def per_device(
    section_inputs, top_grads, weights, norm_gains, feedback, rotation_bits, batch_order
):
    section_count = lax.axis_size("section")
    section_here = lax.axis_index("section")
    micro_count, token_count, width = section_inputs.shape[1:]
    rank = weights.shape[2]
    rows = micro_count * token_count
    chunks = rows // CHUNK
    weight = lax.all_gather(weights[0], "fsdp", axis=0, tiled=True)
    gain_row = lax.all_gather(norm_gains, "fsdp", axis=1, tiled=True)
    above = jnp.minimum(section_here + 1, section_count - 1)
    bits = jnp.stack([rotation_bits[section_here], rotation_bits[above]])
    signs = (1 - 2 * bits).astype(f32)
    x = section_inputs[0][batch_order].reshape(rows, width)
    top = top_grads[batch_order].reshape(rows, width)
    vmem = pl.BlockSpec(memory_space=pltpu.VMEM)
    hbm = pl.BlockSpec(memory_space=pl.ANY)
    gout, dw, gsum, fb_out = pl.pallas_call(
        functools.partial(relay_kernel, section_count),
        out_shape=(
            jax.ShapeDtypeStruct((rows, width), f32),
            jax.ShapeDtypeStruct((width, rank), bf16),
            jax.ShapeDtypeStruct((1, width), f32),
            jax.ShapeDtypeStruct((token_count, width), f32),
        ),
        in_specs=[vmem, hbm, vmem, vmem, vmem, vmem, hbm],
        out_specs=(hbm, vmem, vmem, vmem),
        scratch_shapes=[
            pltpu.VMEM((rows, width + LANES), bf16),
            pltpu.VMEM((SLOTS, CHUNK, width + LANES), bf16),
            pltpu.VMEM((rows, width), bf16),
            pltpu.VMEM((2, CHUNK, width), f32),
            pltpu.VMEM((rows, rank), f32),
            pltpu.VMEM((rows, rank), bf16),
            pltpu.VMEM((rows, rank), bf16),
            pltpu.VMEM((rows, LANES), f32),
            pltpu.VMEM((8, width), f32),
            pltpu.SemaphoreType.DMA((chunks,)),
            pltpu.SemaphoreType.DMA((SLOTS,)),
            pltpu.SemaphoreType.DMA((2,)),
            pltpu.SemaphoreType.DMA,
            pltpu.SemaphoreType.DMA,
        ],
        compiler_params=pltpu.CompilerParams(
            collective_id=0, has_side_effects=True, vmem_limit_bytes=60 * 1024 * 1024
        ),
    )(x, top, weight, gain_row, signs, hadamard(HB).astype(bf16), feedback[0])
    gain_share = lax.psum_scatter(gsum, "fsdp", scatter_dimension=1, tiled=True)
    weight_share = lax.psum_scatter(dw, "fsdp", scatter_dimension=0, tiled=True).astype(f32)
    slot_of = jnp.argmax(batch_order[None, :] == jnp.arange(micro_count)[:, None], axis=1)
    input_grads = gout.reshape(micro_count, token_count, width)[slot_of]
    return (input_grads[None], weight_share[None], gain_share, fb_out[None])


def solution(mesh):
    return jax.shard_map(
        per_device,
        mesh=mesh,
        in_specs=(
            P("section", None, "fsdp", None),
            P(None, "fsdp", None),
            P("section", "fsdp", None),
            P("section", "fsdp"),
            P("section", "fsdp", None),
            P(),
            P(),
        ),
        out_specs=(
            P("section", None, "fsdp", None),
            P("section", "fsdp", None),
            P("section", "fsdp"),
            P("section", "fsdp", None),
        ),
        check_vma=False,
    )
```

time: 984 us -> 561 us (0.57); the launches traced: 972 us -> 560 us
  waiting for transfers between devices: 653 us -> 146 us
  Pallas kernels: 0 us -> 311 us
  matrix products: 86.6 us -> 0 us
  local copies, waits for them, and re-layouts: 92.1 us -> 51.5 us
  other arithmetic: 61 us -> 20.9 us
  blocking collectives: 42.8 us -> 16.4 us
  starting transfers between devices: 12.9 us -> 0.12 us
    ppermute x10 -> x0, waiting for transfers between devices: 448 us -> none  [shifted(): return lax.ppermute(value, axis, pairs)]
    pallas_call x0 -> x1, Pallas kernels: none -> 311 us  [per_device(): pl.pallas_call(functools.partial(relay_kernel, section_count), out_shape=...]
    dot_general x14 -> x0, matrix products: 86.6 us -> none  [the longest x7 50.9 us: restore(): unrotated = jnp.einsum('tbk,kj->tbj', rotated, matrix, precision=highest)]
    reduce_scatter x1, waiting for transfers between devices: 136 us -> 88.3 us  [per_device(): lax.psum_scatter(dw, 'fsdp', scatter_dimension=0, tiled=True).astype(f32)]
    gather x0 -> x9, local copies, waits for them, and re-layouts: none -> 41.7 us  [the longest x3 18.4 us: per_device(): input_grads = gout.reshape(micro_count, token_count, width)[slot_of]]
    all_gather x1, waiting for transfers between devices: 69 us -> 36.7 us  [per_device(): weight = lax.all_gather(weights[0], 'fsdp', axis=0, tiled=True)]
    unnamed x1 -> x0, blocking collectives: 27.1 us -> none
    dynamic_update_slice x6 -> x0, other arithmetic: 26.2 us -> none  [the longest x2 13.2 us: work(): lax.dynamic_update_index_in_dim(hidden_w, hidden_in, micro, 0)]
  transfers between devices with their start and end apart: 12 -> 3, of which waited for: 7 -> 3; matrix products, arithmetic and copies ran while one was open for 0% -> 11% of each run, Pallas kernels for 0% -> 0%
where the time goes in v1:
time: 561 us; the launch traced here: 560 us
  Pallas kernels  311 us (55%)
  waiting for transfers between devices  146 us (26%)
  local copies, waits for them, and re-layouts  51.5 us (9%)
  other arithmetic  20.9 us (4%)
  blocking collectives  16.4 us (3%)
  between operations  13.8 us (2%)
    pallas_call x1, Pallas kernels, per_device(): pl.pallas_call(functools.partial(relay_kernel, section_count), out_shape=...  311 us
    reduce_scatter x1, waiting for transfers between devices, per_device(): lax.psum_scatter(dw, 'fsdp', scatter_dimension=0, tiled=True).astype(f32)  88.3 us
    all_gather x1, waiting for transfers between devices, per_device(): weight = lax.all_gather(weights[0], 'fsdp', axis=0, tiled=True)  36.7 us
    unnamed x4, waiting for transfers between devices  21.2 us
    gather x3, local copies, waits for them, and re-layouts, per_device(): input_grads = gout.reshape(micro_count, token_count, width)[slot_of]  18.4 us
    all_gather x1, blocking collectives, per_device(): gain_row = lax.all_gather(norm_gains, 'fsdp', axis=1, tiled=True)  16.4 us
    gather x3, local copies, waits for them, and re-layouts, per_device(): x = section_inputs[0][batch_order].reshape(rows, width)  12.7 us
  transfers between devices with their start and end apart: 3, of which 3 were waited for; matrix products, arithmetic and copies ran while one was open for 11% of the time, Pallas kernels for 0%

profile of v1, /device:TPU:0, one launch (start us, length us, event | category | flops | bytes accessed | tf_op | source)
XLA Modules:
  0.0 560.0 jit_solution(15761090987235506361)
XLA Ops:
  7.2 0.0 all-gather.3.cloned.1.call-start
  7.2 0.7 all-gather.3.cloned.1.call-update
  7.9 0.0 reduce-scatter.7.cloned.1.call-start
  8.0 1.3 compare_reduce_fusion
  9.2 0.7 compare_select_fusion
  9.9 4.7 fusion.9
  14.6 2.3 gather_fusion.2
  16.9 3.6 gather_fusion.3
  20.5 5.5 fusion.10
  26.0 0.0 copy-start.3
  26.0 0.0 copy-start.2
  26.0 3.6 gather_fusion
  29.6 3.6 gather_fusion.1
  33.2 0.0 copy-done.3
  33.2 16.4 %all_gather.7.gain = f32[1,8192]{1,0:T(1,128)} all-gather(f32[1,1024]{1,0:T(1,128)S(1)} %copy-done.3), channel_id=1, replica_groups=mesh['section'=4,'fsdp'=8] {'fsdp'}, dimensions={1}, use_global_device_ids=true | all-gather | bytes 36864 | tf_op jit(solution)/shard_map/all_gather | solution.py:242
  49.6 1.0 fusion.5.matrix
  50.6 0.0 copy-done.2
  50.6 0.1 constant_dynamic-slice_fusion.1
  50.6 0.7 fusion.7.signs
  51.3 0.0 copy-start
  51.3 0.0 copy-start.1
  51.3 4.1 pad_maximum_fusion.1
  55.4 0.0 copy-done
  55.4 0.0 copy-done.1
  55.4 2.5 pad_maximum_fusion
  57.9 36.7 %all-gather.3.cloned.1.call-done = bf16[1,8192,512]{2,1,0:T(8,128)(2,1)} async-done(((bf16[1,1024,512]{2,1,0:T(8,128)(2,1)}), bf16[1,8192,512]{2,1,0:T(8,128)(2,1)}) %all-gather.3.cloned.1.call-update) | async-done | bytes 8388624 | tf_op jit(solution)/shard_map/all_gather | solution.py:241
  94.6 311.1 %shard_map.102 = (f32[256,8192]{1,0:T(8,128)}, bf16[8192,512]{1,0:T(8,128)(2,1)}, f32[1,8192]{1,0:T(1,128)}, f32[128,8192]{1,0:T(8,128)}) custom-call(bf16[256,8192]{1,0:T(8,128)(2,1)} %bitcast.16, bf16[256,8192]{1,0:T(8,128)(2,1)} %bitcast.15, bf16[8192,512]{1,0:T(8,128)(2,1)} %bitcast.17, f32[1,8192]{1,0:T(1,128)} %all_gather.7.gain, ...), custom_call_target="tpu_custom_call" | custom-call | tf_op jit(solution)/shard_map/pallas_call | solution.py:250
  405.8 3.3 copy.11
  409.1 0.0 reduce-scatter.7.cloned.1.call-update
  409.1 0.0 reduce-scatter.5.cloned.1.call-start
  409.2 0.7 reduce-scatter.5.cloned.1.call-update
  409.9 8.3 %fusion.8 = (f32[2,128,4096]{2,1,0:T(8,128)}, f32[2,128,4096]{2,1,0:T(8,128)}) fusion(f32[2,128,8192]{2,1,0:T(8,128)} %bitcast.18), kind=kLoop, calls=%fused_computation.29 | loop fusion | bytes 16777216 | tf_op jit(solution)/shard_map/gather | solution.py:283
  418.1 5.1 gather_fusion.4
  423.2 5.1 gather_fusion.5
  428.3 7.9 %maximum_bitcast_fusion = f32[1,2,128,8192]{3,2,1,0:T(8,128)} fusion(f32[2,128,4096]{2,1,0:T(8,128)} %gather_fusion.5, f32[2,128,4096]{2,1,0:T(8,128)} %gather_fusion.4), kind=kLoop, calls=%fused_computation.6 | loop fusion | flops 2097152 | bytes 16777216 | tf_op jit(solution)/shard_map/broadcast_in_dim | solution.py:284
  436.2 19.8 %reduce-scatter.7.cloned.1.call-done = f32[1024,1]{1,0:T(8,128)} async-done(((f32[8192,1]{1,0:T(8,128)}), f32[1024,1]{1,0:T(8,128)}) %reduce-scatter.7.cloned.1.call-update) | async-done | bytes 4112
  456.0 1.8 copy.12
  457.8 88.3 %reduce-scatter.5.cloned.1.call-done = bf16[1024,512]{1,0:T(8,128)(2,1)} async-done(((bf16[8192,512]{1,0:T(8,128)(2,1)}), bf16[1024,512]{1,0:T(8,128)(2,1)}) %reduce-scatter.5.cloned.1.call-update) | async-done | bytes 1048592 | tf_op jit(solution)/shard_map/reduce_scatter | solution.py:281
  546.1 2.8 bitcast_convert_fusion
  548.9 4.6 copy.14
  (2 shorter events, 0.0 us)
Async XLA Ops:
  7.2 87.4 %all-gather.3.cloned.1.call-start = ((), (), s32[]{:S(2)}) async-start(), calls=%async_computation.3 | async-start | bytes 9437184 | tf_op jit(solution)/shard_map/all_gather | solution.py:241
  7.9 448.1 %reduce-scatter.7.cloned.1.call-start = ((), (), s32[]{:S(2)}) async-start(), calls=%async_computation.4 | async-start | bytes 4718592
  26.0 7.2 %copy-start.3 = (f32[1,1024]{1,0:T(1,128)S(1)}, f32[1,1024]{1,0:T(1,128)}, u32[]{:S(2)}) copy-start(f32[1,1024]{1,0:T(1,128)} %param.10) | copy-start | bytes 12292
  26.0 24.6 %copy-start.2 = (s32[4,8192]{1,0:T(4,128)S(1)}, s32[4,8192]{1,0:T(4,128)}, u32[]{:S(2)}) copy-start(s32[4,8192]{1,0:T(4,128)} %param.12) | copy-start | bytes 393220
  51.3 4.1 copy-start
  51.3 4.1 copy-start.1
  409.1 136.9 %reduce-scatter.5.cloned.1.call-start = ((), (), s32[]{:S(2)}) async-start(), calls=%async_computation.2 | async-start | bytes 9437184 | tf_op jit(solution)/shard_map/reduce_scatter | solution.py:281
Sparse Core Ops, SparseCore 0:
  9.6 84.9 all-gather.2
  409.2 46.6 reduce-scatter.6
  458.3 87.7 reduce-scatter.4

commit v2 on v1

v2 whole, which is shorter than its diff:
```python
import functools

import jax
import jax.numpy as jnp
from jax import lax
from jax.experimental import pallas as pl
from jax.experimental.pallas import tpu as pltpu
from jax.sharding import PartitionSpec as P

HB = 256
CHUNK = 32
SLOTS = 4
LANES = 128
GROUP = 8
MESH = pl.DeviceIdType.MESH

eps_norm = 1e-05
eps_scale = 1e-06
f32 = jnp.float32
bf16 = jnp.bfloat16


def hadamard(order_size):
    position = jnp.arange(order_size, dtype=jnp.int32)
    shared_bits = jnp.bitwise_and(position[:, None], position[None, :])
    parity = jnp.zeros((order_size, order_size), jnp.int32)
    for bit_place in range(order_size.bit_length() - 1):
        parity = parity + jnp.bitwise_and(jnp.right_shift(shared_bits, bit_place), 1)
    return (1 - 2 * (parity % 2)).astype(f32) / jnp.sqrt(f32(order_size))


def dot(a, b, ca=1, cb=0):
    return lax.dot_general(a, b, (((ca,), (cb,)), ((), ())), preferred_element_type=f32)


def stack(value):
    return jnp.concatenate(
        [value[:, j * HB:(j + 1) * HB] for j in range(value.shape[1] // HB)], axis=0
    )


def unstack(value, rows):
    return jnp.concatenate(
        [value[j * rows:(j + 1) * rows] for j in range(value.shape[0] // rows)], axis=1
    )


def span(index, size):
    return pl.ds(pl.multiple_of(index * size, size), size)


def relay_kernel(
    sections, peers, x, top, weight_in, gain_in, signs, matrix, fb_in,
    gout, dw, gain_out, fb,
    weight, gain, inbox, outbox, hidden, stage, pre, grad_act, right, sinv, gacc,
    gsum, gparts, own_part, sib_out, sib_in, chain_in,
    recv_sem, send_sem, out_sem, fb_sem, top_sem, own_sem,
    w_recv, w_send, g_recv, g_send, s_recv, s_send, b_recv, b_send, c_recv, c_send,
):
    sec = lax.axis_index("section")
    here = lax.axis_index("fsdp")
    chips = peers // 2
    chip = here // 2
    core = lax.rem(here, 2)
    sibling = here + 1 - 2 * core
    rows_all, width = x.shape
    rank = weight.shape[1]
    shard = width // peers
    held = fb.shape[0]
    chunks = rows_all // CHUNK
    last = sections - 1
    wide = 1024
    barrier = pltpu.get_barrier_semaphore()

    for k in range(1, peers):
        pl.semaphore_signal(
            barrier, inc=1, device_id={"fsdp": lax.rem(here + k, peers)}, device_id_type=MESH
        )

    @pl.when(sec < last)
    def _():
        pl.semaphore_signal(barrier, inc=1, device_id={"section": sec + 1}, device_id_type=MESH)

    own_copy = pltpu.make_async_copy(weight_in, weight.at[span(here, shard)], own_sem)
    own_copy.start()
    fb_copy = pltpu.make_async_copy(fb_in, fb, fb_sem)
    fb_copy.start()
    top_copy = pltpu.make_async_copy(top, inbox.at[:, pl.ds(0, width)], top_sem)

    @pl.when(sec == last)
    def _():
        top_copy.start()

    gain[:, span(here, shard)] = gain_in[...]
    gacc[...] = jnp.zeros_like(gacc)
    pre[...] = jnp.zeros_like(pre)
    pl.semaphore_wait(barrier, peers - 1 + (sec > 0).astype(jnp.int32))

    own_copy.wait()

    def weight_copy(owner, target, way):
        return pltpu.make_async_remote_copy(
            src_ref=weight.at[span(owner, shard)],
            dst_ref=weight.at[span(owner, shard)],
            send_sem=w_send.at[way * chips + owner // 2],
            recv_sem=w_recv.at[owner],
            device_id={"fsdp": target},
            device_id_type=MESH,
        )

    def pass_right(owner, act):
        @pl.when(chip < chips - 1)
        def _():
            act(weight_copy(owner, here + 2, 0))

    def pass_left(owner, act):
        @pl.when(chip > 0)
        def _():
            act(weight_copy(owner, here - 2, 1))

    def pass_sibling(owner, act):
        act(weight_copy(owner, sibling, 2))

    def start(copy):
        copy.start()

    def finish(copy):
        copy.wait_send()

    def gain_copy(k):
        return pltpu.make_async_remote_copy(
            src_ref=gain.at[:, span(here, shard)],
            dst_ref=gain.at[:, span(here, shard)],
            send_sem=g_send.at[k],
            recv_sem=g_recv.at[k],
            device_id={"fsdp": lax.rem(here + k, peers)},
            device_id_type=MESH,
        )

    for k in range(1, peers):
        gain_copy(k).start()
    pass_right(here, start)
    pass_left(here, start)
    pass_sibling(here, start)

    @pl.loop(0, chunks)
    def _(c):
        rows = span(c, CHUNK)

        def square(k, acc):
            part = x[rows, span(k, wide)].astype(f32)
            part = part * part
            for j in range(wide // LANES):
                acc = acc + part[:, j * LANES:(j + 1) * LANES]
            return acc

        acc = lax.fori_loop(0, width // wide, square, jnp.zeros((CHUNK, LANES), f32))
        scale_inv = lax.rsqrt(jnp.sum(acc, axis=-1, keepdims=True) / width + eps_norm)
        sinv[rows, :] = jnp.broadcast_to(scale_inv, (CHUNK, LANES))

    for k in range(1, peers):
        pltpu.make_async_remote_copy(
            src_ref=gain.at[:, span(here, shard)],
            dst_ref=gain.at[:, span(lax.rem(here + peers - k, peers), shard)],
            send_sem=g_send.at[k],
            recv_sem=g_recv.at[k],
            device_id={"fsdp": lax.rem(here + k, peers)},
            device_id_type=MESH,
        ).wait_recv()

    @pl.loop(0, chunks)
    def _(c):
        rows = span(c, CHUNK)
        scale_inv = sinv[rows, 0:1]

        @pl.loop(0, width // wide)
        def _(k):
            cols = span(k, wide)
            hidden[rows, cols] = (x[rows, cols].astype(f32) * scale_inv * gain[:, cols]).astype(bf16)

    def accumulate(spot):
        other = spot * 2 + 1 - core
        weight_copy(other, sibling, 2).wait_recv()
        for owner in (spot * 2 + core, other):
            cols = span(owner, shard)
            pre[...] += dot(hidden[:, cols], weight[cols, :])

    def accumulate_around(distance):
        @pl.when(chip >= distance)
        def _():
            accumulate(chip - distance)

        if distance > 0:
            @pl.when(chip + distance < chips)
            def _():
                accumulate(chip + distance)

    for distance in range(1, chips):
        @pl.when(chip >= distance)
        def _():
            owner = here - 2 * distance
            weight_copy(owner, sibling, 2).wait_recv()
            pass_right(owner, start)
            pass_sibling(owner, start)

        @pl.when(chip + distance < chips)
        def _():
            owner = here + 2 * distance
            weight_copy(owner, sibling, 2).wait_recv()
            pass_left(owner, start)
            pass_sibling(owner, start)

        accumulate_around(distance - 1)
    accumulate_around(chips - 1)

    fb_copy.wait()

    @pl.when(sec == last)
    def _():
        top_copy.wait()

    lane = lax.broadcasted_iota(jnp.int32, (CHUNK, LANES), 1)
    group_wide = GROUP * HB
    groups = width // group_wide

    def send(c, slot):
        return pltpu.make_async_remote_copy(
            src_ref=outbox.at[slot],
            dst_ref=inbox.at[span(c, CHUNK)],
            send_sem=send_sem.at[slot],
            recv_sem=recv_sem.at[c],
            device_id={"section": sec - 1},
            device_id_type=MESH,
        )

    def store(c, half):
        return pltpu.make_async_copy(stage.at[half], gout.at[span(c, CHUNK)], out_sem.at[half])

    @pl.loop(0, chunks)
    def _(c):
        rows = span(c, CHUNK)
        kept = span(lax.rem(c, held // CHUNK), CHUNK)
        half = lax.rem(c, 2)
        slot = lax.rem(c, SLOTS)

        @pl.when(c >= 2)
        def _():
            store(c - 2, half).wait()

        @pl.when(sec == last)
        def _():
            def multiply(k, acc):
                cols = span(k, group_wide)
                value = inbox[rows, cols]
                stage[half, :, cols] = value.astype(f32)
                return acc + dot(value, weight[cols, :])

            grad_act[...] = lax.fori_loop(0, groups, multiply, jnp.zeros((CHUNK, rank), f32))

        @pl.when(sec < last)
        def _():
            send(c, slot).wait_recv()
            scales = inbox[rows, pl.ds(width, LANES)].astype(f32)

            def decode(k, acc):
                cols = span(k, group_wide)
                scale = jnp.concatenate([
                    jnp.sum(jnp.where(lane == k * GROUP + j, scales, 0.0), axis=-1, keepdims=True)
                    for j in range(GROUP)
                ], axis=0)
                value = dot(stack(inbox[rows, cols]), matrix[...]) * scale
                value = unstack(value, CHUNK) * signs[1:2, cols]
                low = value.astype(bf16)
                stage[half, :, cols] = value
                inbox[rows, cols] = low
                return acc + dot(low, weight[cols, :])

            grad_act[...] = lax.fori_loop(0, groups, decode, jnp.zeros((CHUNK, rank), f32))

        pre_here = pre[rows, :]
        sigma = jax.nn.sigmoid(pre_here)
        grad_pre = (grad_act[...] * sigma * (1.0 + pre_here * (1.0 - sigma))).astype(bf16)
        right[rows, :] = grad_pre
        right[span(c + chunks, CHUNK), :] = (pre_here * sigma).astype(bf16)
        inner = jnp.sum(grad_pre.astype(f32) * pre_here, axis=-1, keepdims=True) / width
        scale_inv = sinv[rows, 0:1]

        def layer_block(cols):
            grad_hidden = dot(grad_pre, weight[cols, :], 1, 1)
            normed = x[rows, cols].astype(f32) * scale_inv
            term = grad_hidden * normed
            total = term[0:8]
            for j in range(1, CHUNK // 8):
                total = total + term[8 * j:8 * j + 8]
            grad_out = stage[half, :, cols] + scale_inv * (grad_hidden * gain[:, cols] - normed * inner)
            return total, grad_out

        @pl.when(sec == 0)
        def _():
            @pl.loop(0, groups)
            def _(k):
                cols = span(k, group_wide)
                total, grad_out = layer_block(cols)
                gacc[:, cols] += total
                stage[half, :, cols] = grad_out

        @pl.when(sec > 0)
        def _():
            @pl.when(c >= SLOTS)
            def _():
                send(c - SLOTS, slot).wait_send()

            def encode(k, scales):
                cols = span(k, group_wide)
                total, grad_out = layer_block(cols)
                value = grad_out + fb[kept, cols]
                sign = signs[0:1, cols]
                turned = stack(value * sign)
                high = turned.astype(bf16)
                low = (turned - high.astype(f32)).astype(bf16)
                rotated = dot(jnp.concatenate([high, low], axis=0), matrix[...])
                rotated = rotated[:GROUP * CHUNK] + rotated[GROUP * CHUNK:]
                scale = jnp.sum(jnp.abs(rotated), axis=-1, keepdims=True) / HB + eps_scale
                scale = scale.astype(bf16).astype(f32)
                levels = jnp.clip(rotated * (1.0 / scale), -1.0, 1.0).astype(bf16)
                decoded = unstack(dot(levels, matrix[...]) * scale, CHUNK) * sign
                gacc[:, cols] += total
                stage[half, :, cols] = grad_out
                outbox[slot, :, cols] = unstack(levels, CHUNK)
                fb[kept, cols] = value - decoded
                for j in range(GROUP):
                    scales = jnp.where(
                        lane == k * GROUP + j, scale[j * CHUNK:(j + 1) * CHUNK], scales
                    )
                return scales

            scales = lax.fori_loop(0, groups, encode, jnp.zeros((CHUNK, LANES), f32))
            outbox[slot, :, pl.ds(width, LANES)] = scales.astype(bf16)
            send(c, slot).start()

        store(c, half).start()

    gsum[...] = jnp.sum(gacc[...], axis=0, keepdims=True)

    def sum_copy(k):
        target = lax.rem(here + k, peers)
        return pltpu.make_async_remote_copy(
            src_ref=gsum.at[:, span(target, shard)],
            dst_ref=gparts.at[k],
            send_sem=s_send.at[k],
            recv_sem=s_recv.at[k],
            device_id={"fsdp": target},
            device_id_type=MESH,
        )

    for k in range(1, peers):
        sum_copy(k).start()

    piece = 256

    def share(owner, into, spot):
        @pl.loop(0, shard // piece)
        def _(k):
            cols = pl.ds(pl.multiple_of(owner * shard + k * piece, piece), piece)
            left = jnp.concatenate([hidden[:, cols], inbox[:, cols]], axis=0)
            into[spot, span(k, piece), :] = dot(left, right[...], 0, 0).astype(bf16)

    def sibling_copy(spot):
        return pltpu.make_async_remote_copy(
            src_ref=sib_out.at[spot],
            dst_ref=sib_in.at[spot],
            send_sem=b_send.at[spot],
            recv_sem=b_recv.at[spot],
            device_id={"fsdp": sibling},
            device_id_type=MESH,
        )

    @pl.loop(0, chips)
    def _(k):
        low_half = (chip < chips // 2).astype(jnp.int32)
        spot = low_half * (chips - 1 - k) + (1 - low_half) * k
        share(spot * 2 + 1 - core, sib_out, spot)
        sibling_copy(spot).start()
        share(spot * 2 + core, own_part, spot)

    def chain_copy(spot, way):
        arrive = spot
        target = here + 2
        if way == 1:
            target = here - 2
            arrive = spot + (chips - spot) * (chip - 1 == spot).astype(jnp.int32)
        return pltpu.make_async_remote_copy(
            src_ref=own_part.at[spot],
            dst_ref=chain_in.at[arrive],
            send_sem=c_send.at[spot],
            recv_sem=c_recv.at[arrive],
            device_id={"fsdp": target},
            device_id_type=MESH,
        )

    def arrived(slot):
        pltpu.make_async_remote_copy(
            src_ref=own_part.at[0],
            dst_ref=chain_in.at[slot],
            send_sem=c_send.at[0],
            recv_sem=c_recv.at[slot],
            device_id={"fsdp": sibling},
            device_id_type=MESH,
        ).wait_recv()

    def merge(spot, inner_chip):
        sibling_copy(spot).wait_recv()

        @pl.when(inner_chip)
        def _():
            arrived(spot)

            @pl.loop(0, shard // piece)
            def _(k):
                part = span(k, piece)
                own_part[spot, part, :] = (
                    own_part[spot, part, :].astype(f32) + sib_in[spot, part, :].astype(f32)
                    + chain_in[spot, part, :].astype(f32)
                ).astype(bf16)

        @pl.when(jnp.logical_not(inner_chip))
        def _():
            @pl.loop(0, shard // piece)
            def _(k):
                part = span(k, piece)
                own_part[spot, part, :] = (
                    own_part[spot, part, :].astype(f32) + sib_in[spot, part, :].astype(f32)
                ).astype(bf16)

    def go_right(k):
        spot = chips - 1 - k

        @pl.when(spot > chip)
        def _():
            merge(spot, chip > 0)
            chain_copy(spot, 0).start()

    def go_left(k):
        @pl.when(k < chip)
        def _():
            merge(k, chip < chips - 1)
            chain_copy(k, 1).start()

    @pl.loop(0, chips)
    def _(k):
        @pl.when(chip < chips // 2)
        def _():
            go_right(k)
            go_left(k)

        @pl.when(chip >= chips // 2)
        def _():
            go_left(k)
            go_right(k)

    sibling_copy(chip).wait_recv()

    @pl.loop(0, shard // piece)
    def _(k):
        part = span(k, piece)
        dw[part, :] = own_part[chip, part, :].astype(f32) + sib_in[chip, part, :].astype(f32)

    def add_arrived(slot):
        arrived(slot)

        @pl.loop(0, shard // piece)
        def _(k):
            part = span(k, piece)
            dw[part, :] += chain_in[slot, part, :].astype(f32)

    @pl.when(chip > 0)
    def _():
        add_arrived(chip)

    @pl.when(chip < chips - 1)
    def _():
        add_arrived(chips)

    total = gsum[:, span(here, shard)]
    for k in range(1, peers):
        sum_copy(k).wait_recv()
        total = total + gparts[k]
    gain_out[...] = total

    for c in range(max(0, chunks - 2), chunks):
        store(c, c % 2).wait()

    @pl.when(sec > 0)
    def _():
        for c in range(max(0, chunks - SLOTS), chunks):
            send(c, c % SLOTS).wait_send()

    for k in range(1, peers):
        gain_copy(k).wait_send()
        sum_copy(k).wait_send()
    pass_right(here, finish)
    pass_left(here, finish)
    pass_sibling(here, finish)
    for distance in range(1, chips):
        @pl.when(chip >= distance)
        def _():
            pass_right(here - 2 * distance, finish)
            pass_sibling(here - 2 * distance, finish)

        @pl.when(chip + distance < chips)
        def _():
            pass_left(here + 2 * distance, finish)
            pass_sibling(here + 2 * distance, finish)

    @pl.loop(0, chips)
    def _(k):
        sibling_copy(k).wait_send()

        @pl.when(k > chip)
        def _():
            chain_copy(k, 0).wait_send()

        @pl.when(k < chip)
        def _():
            chain_copy(k, 1).wait_send()


def reorder_kernel(scatter, order, *refs):
    count = (len(refs) - 1) // 2
    sem = refs[-1]
    copies = []
    for i in range(count):
        source, target = refs[i], refs[count + i]
        pieces = 4
        rows = source.shape[1] // pieces
        for m in range(source.shape[0]):
            for j in range(pieces):
                part = pl.ds(j * rows, rows)
                a, b = (m, order[m]) if scatter else (order[m], m)
                copies.append(
                    pltpu.make_async_copy(source.at[a, part], target.at[b, part], sem.at[len(copies)])
                )
    for copy in copies:
        copy.start()
    for copy in copies:
        copy.wait()


def reorder(order, arrays, scatter):
    hbm = pl.BlockSpec(memory_space=pl.ANY)
    return pl.pallas_call(
        functools.partial(reorder_kernel, scatter),
        out_shape=tuple(jax.ShapeDtypeStruct(a.shape, a.dtype) for a in arrays),
        in_specs=[pl.BlockSpec(memory_space=pltpu.SMEM)] + [hbm] * len(arrays),
        out_specs=(hbm,) * len(arrays),
        scratch_shapes=[pltpu.SemaphoreType.DMA((4 * len(arrays) * arrays[0].shape[0],))],
    )(order, *arrays)


def per_device(
    section_inputs, top_grads, weights, norm_gains, feedback, rotation_bits, batch_order
):
    section_count = lax.axis_size("section")
    peers = lax.axis_size("fsdp")
    section_here = lax.axis_index("section")
    micro_count, token_count, width = section_inputs.shape[1:]
    shard, rank = weights.shape[1:]
    rows = micro_count * token_count
    chunks = rows // CHUNK
    chips = peers // 2
    above = jnp.minimum(section_here + 1, section_count - 1)
    bits = jnp.stack([rotation_bits[section_here], rotation_bits[above]])
    signs = (1 - 2 * bits).astype(f32)
    x, top = reorder(batch_order, (section_inputs[0], top_grads), False)
    vmem = pl.BlockSpec(memory_space=pltpu.VMEM)
    hbm = pl.BlockSpec(memory_space=pl.ANY)
    dma = pltpu.SemaphoreType.DMA
    gout, dw, gain_share, fb_out = pl.pallas_call(
        functools.partial(relay_kernel, section_count, peers),
        out_shape=(
            jax.ShapeDtypeStruct((rows, width), f32),
            jax.ShapeDtypeStruct((shard, rank), f32),
            jax.ShapeDtypeStruct((1, shard), f32),
            jax.ShapeDtypeStruct((token_count, width), f32),
        ),
        in_specs=[vmem, hbm, hbm, vmem, vmem, vmem, hbm],
        out_specs=(hbm, vmem, vmem, vmem),
        scratch_shapes=[
            pltpu.VMEM((width, rank), bf16),
            pltpu.VMEM((1, width), f32),
            pltpu.VMEM((rows, width + LANES), bf16),
            pltpu.VMEM((SLOTS, CHUNK, width + LANES), bf16),
            pltpu.VMEM((rows, width), bf16),
            pltpu.VMEM((2, CHUNK, width), f32),
            pltpu.VMEM((rows, rank), f32),
            pltpu.VMEM((CHUNK, rank), f32),
            pltpu.VMEM((2 * rows, rank), bf16),
            pltpu.VMEM((rows, LANES), f32),
            pltpu.VMEM((8, width), f32),
            pltpu.VMEM((1, width), f32),
            pltpu.VMEM((peers, 1, shard), f32),
            pltpu.VMEM((chips, shard, rank), bf16),
            pltpu.VMEM((chips, shard, rank), bf16),
            pltpu.VMEM((chips, shard, rank), bf16),
            pltpu.VMEM((chips + 1, shard, rank), bf16),
            dma((chunks,)), dma((SLOTS,)), dma((2,)), dma, dma, dma,
            dma((peers,)), dma((3 * chips,)),
            dma((peers,)), dma((peers,)),
            dma((peers,)), dma((peers,)),
            dma((chips,)), dma((chips,)),
            dma((chips + 1,)), dma((chips,)),
        ],
        compiler_params=pltpu.CompilerParams(
            collective_id=0, has_side_effects=True, vmem_limit_bytes=60 * 1024 * 1024
        ),
    )(
        x.reshape(rows, width), top.reshape(rows, width), weights[0], norm_gains, signs,
        hadamard(HB).astype(bf16), feedback[0],
    )
    (input_grads,) = reorder(batch_order, (gout.reshape(micro_count, token_count, width),), True)
    return (input_grads[None], dw[None], gain_share, fb_out[None])


def solution(mesh):
    return jax.shard_map(
        per_device,
        mesh=mesh,
        in_specs=(
            P("section", None, "fsdp", None),
            P(None, "fsdp", None),
            P("section", "fsdp", None),
            P("section", "fsdp"),
            P("section", "fsdp", None),
            P(),
            P(),
        ),
        out_specs=(
            P("section", None, "fsdp", None),
            P("section", "fsdp", None),
            P("section", "fsdp"),
            P("section", "fsdp", None),
        ),
        check_vma=False,
    )
```

time: 561 us -> 836 us (1.49)
  Pallas kernels: 311 us -> 827 us
  waiting for transfers between devices: 146 us -> 0 us
  local copies, waits for them, and re-layouts: 51.5 us -> 6 us
  other arithmetic: 20.9 us -> 1.69 us
  blocking collectives: 16.4 us -> 0 us
  between operations: 13.8 us -> 0.7 us
    pallas_call x1 -> x3, Pallas kernels: 311 us -> 827 us  [the longest x2 512 us: reorder(): pl.pallas_call(functools.partial(reorder_kernel, scatter), out_shape=tupl...]
    reduce_scatter x1 -> x0, waiting for transfers between devices: 88.3 us -> none  [per_device(): lax.psum_scatter(dw, 'fsdp', scatter_dimension=0, tiled=True).astype(f32)]
    gather x9 -> x0, local copies, waits for them, and re-layouts: 41.7 us -> none  [the longest x3 18.4 us: per_device(): input_grads = gout.reshape(micro_count, token_count, width)[slot_of]]
    all_gather x1 -> x0, waiting for transfers between devices: 36.7 us -> none  [per_device(): weight = lax.all_gather(weights[0], 'fsdp', axis=0, tiled=True)]
    unnamed x4 -> x0, waiting for transfers between devices: 21.2 us -> none
    all_gather x1 -> x0, blocking collectives: 16.4 us -> none  [per_device(): gain_row = lax.all_gather(norm_gains, 'fsdp', axis=1, tiled=True)]
    broadcast_in_dim x2 -> x0, other arithmetic: 10.7 us -> none  [per_device(): return (input_grads[None], weight_share[None], gain_share, fb_out[None])]
  transfers between devices with their start and end apart: 3 -> 0, of which waited for: 3 -> 0; matrix products, arithmetic and copies ran while one was open for 11% -> 0% of each run, Pallas kernels for 0% -> 0%
where the time goes in v2:
time: 836 us; the launch traced here: 835 us
  Pallas kernels  827 us (99%)
    pallas_call x2, Pallas kernels, reorder(): pl.pallas_call(functools.partial(reorder_kernel, scatter), out_shape=tupl...  512 us
    pallas_call x1, Pallas kernels, per_device(): pl.pallas_call(functools.partial(relay_kernel, section_count, peers), out...  315 us

profile of v2, /device:TPU:0, one launch (start us, length us, event | category | flops | bytes accessed | tf_op | source)
XLA Modules:
  0.0 835.3 jit_solution(4211083606602614299)
XLA Ops:
  0.6 1.1 constant_dynamic-slice_fusion.1
  1.7 0.7 fusion.7.signs
  2.4 1.0 fusion.5.matrix
  3.4 256.0 %shard_map.102 = (bf16[2,128,8192]{2,1,0:T(8,128)(2,1)}, bf16[2,128,8192]{2,1,0:T(8,128)(2,1)}) custom-call(s32[2]{0:T(128)} %order.3, bf16[2,128,8192]{2,1,0:T(8,128)(2,1)} %bitcast.11, bf16[2,128,8192]{2,1,0:T(8,128)(2,1)} %refs_1_.1), custom_call_target="tpu_custom_call" | custom-call | tf_op jit(solution)/shard_map/pallas_call | solution.py:551
  259.4 314.9 %shard_map.103 = (f32[256,8192]{1,0:T(8,128)}, f32[1024,512]{1,0:T(8,128)}, f32[1,1024]{1,0:T(1,128)}, f32[128,8192]{1,0:T(8,128)}) custom-call(bf16[256,8192]{1,0:T(8,128)(2,1)} %bitcast.14, bf16[256,8192]{1,0:T(8,128)(2,1)} %bitcast.15, bf16[1024,512]{1,0:T(8,128)(2,1)} %bitcast.17, f32[1,1024]{1,0:T(1,128)} %gain_in.1, f32[2,8192]{1,0:T(2,128)} %fusion.7.signs, ...), custom_call_target="tpu_custom_call" | custom-call | tf_op jit(solution)/shard_map/pallas_call | solution.py:578
  574.3 0.0 copy-start.1
  574.3 0.0 copy-start.2
  574.3 256.1 %shard_map.104 = f32[2,128,8192]{2,1,0:T(8,128)} custom-call(s32[2]{0:T(128)} %order.3, f32[2,128,8192]{2,1,0:T(8,128)} %bitcast.10), custom_call_target="tpu_custom_call" | custom-call | tf_op jit(solution)/shard_map/pallas_call | solution.py:551
  830.4 0.0 copy-start
  830.4 0.0 copy-done.1
  830.4 1.3 copy.14
  831.7 0.0 copy-done.2
  831.7 0.6 copy.15
  832.3 1.0 copy-done
  833.3 2.0 copy.16
Async XLA Ops:
  574.3 256.1 %copy-start.1 = (f32[1024,512]{1,0:T(8,128)S(1)}, f32[1024,512]{1,0:T(8,128)}, u32[]{:S(2)}) copy-start(f32[1024,512]{1,0:T(8,128)} %get-tuple-element.13) | copy-start | bytes 6291460
  574.3 257.4 %copy-start.2 = (f32[1,1024]{1,0:T(1,128)S(1)}, f32[1,1024]{1,0:T(1,128)}, u32[]{:S(2)}) copy-start(f32[1,1024]{1,0:T(1,128)} %get-tuple-element.24) | copy-start | bytes 12292
  830.4 2.9 copy-start

commit v3 on v2

--- a/solution.py
+++ b/solution.py
@@ -85,15 +85,26 @@
     own_copy.start()
     fb_copy = pltpu.make_async_copy(fb_in, fb, fb_sem)
     fb_copy.start()
-    top_copy = pltpu.make_async_copy(top, inbox.at[:, pl.ds(0, width)], top_sem)
+    group_wide = GROUP * HB
+    groups = width // group_wide
+    top_copies = [
+        pltpu.make_async_copy(
+            top.at[:, pl.ds(k * group_wide, group_wide)],
+            inbox.at[k, :, pl.ds(0, group_wide)],
+            top_sem.at[k],
+        )
+        for k in range(groups)
+    ]
 
     @pl.when(sec == last)
     def _():
-        top_copy.start()
+        for copy in top_copies:
+            copy.start()
 
     gain[:, span(here, shard)] = gain_in[...]
     gacc[...] = jnp.zeros_like(gacc)
     pre[...] = jnp.zeros_like(pre)
+    grad_act[...] = jnp.zeros_like(grad_act)
     pl.semaphore_wait(barrier, peers - 1 + (sec > 0).astype(jnp.int32))
 
     own_copy.wait()
@@ -178,6 +189,11 @@
             cols = span(k, wide)
             hidden[rows, cols] = (x[rows, cols].astype(f32) * scale_inv * gain[:, cols]).astype(bf16)
 
+    @pl.when(sec == last)
+    def _():
+        for copy in top_copies:
+            copy.wait()
+
     def accumulate(spot):
         other = spot * 2 + 1 - core
         weight_copy(other, sibling, 2).wait_recv()
@@ -185,6 +201,12 @@
             cols = span(owner, shard)
             pre[...] += dot(hidden[:, cols], weight[cols, :])
 
+            @pl.when(sec == last)
+            def _():
+                first = owner * shard
+                part = pl.ds(pl.multiple_of(lax.rem(first, group_wide), shard), shard)
+                grad_act[...] += dot(inbox[first // group_wide, :, part], weight[cols, :])
+
     def accumulate_around(distance):
         @pl.when(chip >= distance)
         def _():
@@ -214,21 +236,14 @@
     accumulate_around(chips - 1)
 
     fb_copy.wait()
-
-    @pl.when(sec == last)
-    def _():
-        top_copy.wait()
-
     lane = lax.broadcasted_iota(jnp.int32, (CHUNK, LANES), 1)
-    group_wide = GROUP * HB
-    groups = width // group_wide
-
-    def send(c, slot):
+
+    def send(c, slot, k):
         return pltpu.make_async_remote_copy(
-            src_ref=outbox.at[slot],
-            dst_ref=inbox.at[span(c, CHUNK)],
-            send_sem=send_sem.at[slot],
-            recv_sem=recv_sem.at[c],
+            src_ref=outbox.at[slot, k],
+            dst_ref=inbox.at[k, span(c, CHUNK)],
+            send_sem=send_sem.at[slot, k],
+            recv_sem=recv_sem.at[c, k],
             device_id={"section": sec - 1},
             device_id_type=MESH,
         )
@@ -249,37 +264,29 @@
 
         @pl.when(sec == last)
         def _():
-            def multiply(k, acc):
-                cols = span(k, group_wide)
-                value = inbox[rows, cols]
-                stage[half, :, cols] = value.astype(f32)
-                return acc + dot(value, weight[cols, :])
-
-            grad_act[...] = lax.fori_loop(0, groups, multiply, jnp.zeros((CHUNK, rank), f32))
+            @pl.loop(0, groups)
+            def _(k):
+                stage[half, :, span(k, group_wide)] = inbox[k, rows, pl.ds(0, group_wide)].astype(f32)
 
         @pl.when(sec < last)
         def _():
-            send(c, slot).wait_recv()
-            scales = inbox[rows, pl.ds(width, LANES)].astype(f32)
-
             def decode(k, acc):
                 cols = span(k, group_wide)
-                scale = jnp.concatenate([
-                    jnp.sum(jnp.where(lane == k * GROUP + j, scales, 0.0), axis=-1, keepdims=True)
-                    for j in range(GROUP)
-                ], axis=0)
-                value = dot(stack(inbox[rows, cols]), matrix[...]) * scale
+                send(c, slot, k).wait_recv()
+                scales = inbox[k, rows, pl.ds(group_wide, LANES)].astype(f32)
+                scale = jnp.concatenate([scales[:, j:j + 1] for j in range(GROUP)], axis=0)
+                value = dot(stack(inbox[k, rows, pl.ds(0, group_wide)]), matrix[...]) * scale
                 value = unstack(value, CHUNK) * signs[1:2, cols]
                 low = value.astype(bf16)
                 stage[half, :, cols] = value
-                inbox[rows, cols] = low
+                inbox[k, rows, pl.ds(0, group_wide)] = low
                 return acc + dot(low, weight[cols, :])
 
-            grad_act[...] = lax.fori_loop(0, groups, decode, jnp.zeros((CHUNK, rank), f32))
+            grad_act[rows, :] = lax.fori_loop(0, groups, decode, jnp.zeros((CHUNK, rank), f32))
 
         pre_here = pre[rows, :]
         sigma = jax.nn.sigmoid(pre_here)
-        grad_pre = (grad_act[...] * sigma * (1.0 + pre_here * (1.0 - sigma))).astype(bf16)
+        grad_pre = (grad_act[rows, :] * sigma * (1.0 + pre_here * (1.0 - sigma))).astype(bf16)
         right[rows, :] = grad_pre
         right[span(c + chunks, CHUNK), :] = (pre_here * sigma).astype(bf16)
         inner = jnp.sum(grad_pre.astype(f32) * pre_here, axis=-1, keepdims=True) / width
@@ -308,9 +315,11 @@
         def _():
             @pl.when(c >= SLOTS)
             def _():
-                send(c - SLOTS, slot).wait_send()
-
-            def encode(k, scales):
+                for k in range(groups):
+                    send(c - SLOTS, slot, k).wait_send()
+
+            @pl.loop(0, groups)
+            def _(k):
                 cols = span(k, group_wide)
                 total, grad_out = layer_block(cols)
                 value = grad_out + fb[kept, cols]
@@ -326,17 +335,13 @@
                 decoded = unstack(dot(levels, matrix[...]) * scale, CHUNK) * sign
                 gacc[:, cols] += total
                 stage[half, :, cols] = grad_out
-                outbox[slot, :, cols] = unstack(levels, CHUNK)
+                outbox[slot, k, :, pl.ds(0, group_wide)] = unstack(levels, CHUNK)
+                scales = jnp.zeros((CHUNK, LANES), f32)
+                for j in range(GROUP):
+                    scales = jnp.where(lane == j, scale[j * CHUNK:(j + 1) * CHUNK], scales)
+                outbox[slot, k, :, pl.ds(group_wide, LANES)] = scales.astype(bf16)
+                send(c, slot, k).start()
                 fb[kept, cols] = value - decoded
-                for j in range(GROUP):
-                    scales = jnp.where(
-                        lane == k * GROUP + j, scale[j * CHUNK:(j + 1) * CHUNK], scales
-                    )
-                return scales
-
-            scales = lax.fori_loop(0, groups, encode, jnp.zeros((CHUNK, LANES), f32))
-            outbox[slot, :, pl.ds(width, LANES)] = scales.astype(bf16)
-            send(c, slot).start()
 
         store(c, half).start()
 
@@ -362,7 +367,9 @@
         @pl.loop(0, shard // piece)
         def _(k):
             cols = pl.ds(pl.multiple_of(owner * shard + k * piece, piece), piece)
-            left = jnp.concatenate([hidden[:, cols], inbox[:, cols]], axis=0)
+            first = owner * shard + k * piece
+            part = pl.ds(pl.multiple_of(lax.rem(first, group_wide), piece), piece)
+            left = jnp.concatenate([hidden[:, cols], inbox[first // group_wide, :, part]], axis=0)
             into[spot, span(k, piece), :] = dot(left, right[...], 0, 0).astype(bf16)
 
     def sibling_copy(spot):
@@ -374,14 +381,6 @@
             device_id={"fsdp": sibling},
             device_id_type=MESH,
         )
-
-    @pl.loop(0, chips)
-    def _(k):
-        low_half = (chip < chips // 2).astype(jnp.int32)
-        spot = low_half * (chips - 1 - k) + (1 - low_half) * k
-        share(spot * 2 + 1 - core, sib_out, spot)
-        sibling_copy(spot).start()
-        share(spot * 2 + core, own_part, spot)
 
     def chain_copy(spot, way):
         arrive = spot
@@ -448,12 +447,28 @@
 
     @pl.loop(0, chips)
     def _(k):
-        @pl.when(chip < chips // 2)
+        low_half = (chip < chips // 2).astype(jnp.int32)
+        spot = low_half * (chips - 1 - k) + (1 - low_half) * k
+        share(spot * 2 + 1 - core, sib_out, spot)
+        sibling_copy(spot).start()
+        share(spot * 2 + core, own_part, spot)
+
+        @pl.when(jnp.logical_and(chip == 0, k > 0))
+        def _():
+            go_right(k - 1)
+
+        @pl.when(jnp.logical_and(chip == chips - 1, k > 0))
+        def _():
+            go_left(k - 1)
+
+    @pl.loop(0, chips)
+    def _(k):
+        @pl.when(jnp.logical_and(chip > 0, chip < chips // 2))
         def _():
             go_right(k)
             go_left(k)
 
-        @pl.when(chip >= chips // 2)
+        @pl.when(jnp.logical_and(chip >= chips // 2, chip < chips - 1))
         def _():
             go_left(k)
             go_right(k)
@@ -493,7 +508,8 @@
     @pl.when(sec > 0)
     def _():
         for c in range(max(0, chunks - SLOTS), chunks):
-            send(c, c % SLOTS).wait_send()
+            for k in range(groups):
+                send(c, c % SLOTS, k).wait_send()
 
     for k in range(1, peers):
         gain_copy(k).wait_send()
@@ -525,35 +541,27 @@
             chain_copy(k, 1).wait_send()
 
 
-def reorder_kernel(scatter, order, *refs):
-    count = (len(refs) - 1) // 2
-    sem = refs[-1]
-    copies = []
-    for i in range(count):
-        source, target = refs[i], refs[count + i]
-        pieces = 4
-        rows = source.shape[1] // pieces
-        for m in range(source.shape[0]):
-            for j in range(pieces):
-                part = pl.ds(j * rows, rows)
-                a, b = (m, order[m]) if scatter else (order[m], m)
-                copies.append(
-                    pltpu.make_async_copy(source.at[a, part], target.at[b, part], sem.at[len(copies)])
-                )
-    for copy in copies:
-        copy.start()
-    for copy in copies:
-        copy.wait()
+def reorder_kernel(order, *refs):
+    count = len(refs) // 2
+    for source, target in zip(refs[:count], refs[count:]):
+        target[...] = source[...]
 
 
 def reorder(order, arrays, scatter):
-    hbm = pl.BlockSpec(memory_space=pl.ANY)
+    micro_count, token_count, width = arrays[0].shape
+    rows = 32
+    straight = pl.BlockSpec((1, rows, width), lambda m, i, order: (m, i, 0))
+    picked = pl.BlockSpec((1, rows, width), lambda m, i, order: (order[m], i, 0))
+    source, target = (straight, picked) if scatter else (picked, straight)
     return pl.pallas_call(
-        functools.partial(reorder_kernel, scatter),
+        reorder_kernel,
         out_shape=tuple(jax.ShapeDtypeStruct(a.shape, a.dtype) for a in arrays),
-        in_specs=[pl.BlockSpec(memory_space=pltpu.SMEM)] + [hbm] * len(arrays),
-        out_specs=(hbm,) * len(arrays),
-        scratch_shapes=[pltpu.SemaphoreType.DMA((4 * len(arrays) * arrays[0].shape[0],))],
+        grid_spec=pltpu.PrefetchScalarGridSpec(
+            num_scalar_prefetch=1,
+            grid=(micro_count, token_count // rows),
+            in_specs=[source] * len(arrays),
+            out_specs=(target,) * len(arrays),
+        ),
     )(order, *arrays)
 
 
@@ -568,6 +576,7 @@
     rows = micro_count * token_count
     chunks = rows // CHUNK
     chips = peers // 2
+    groups = width // (GROUP * HB)
     above = jnp.minimum(section_here + 1, section_count - 1)
     bits = jnp.stack([rotation_bits[section_here], rotation_bits[above]])
     signs = (1 - 2 * bits).astype(f32)
@@ -588,12 +597,12 @@
         scratch_shapes=[
             pltpu.VMEM((width, rank), bf16),
             pltpu.VMEM((1, width), f32),
-            pltpu.VMEM((rows, width + LANES), bf16),
-            pltpu.VMEM((SLOTS, CHUNK, width + LANES), bf16),
+            pltpu.VMEM((groups, rows, GROUP * HB + LANES), bf16),
+            pltpu.VMEM((SLOTS, groups, CHUNK, GROUP * HB + LANES), bf16),
             pltpu.VMEM((rows, width), bf16),
             pltpu.VMEM((2, CHUNK, width), f32),
             pltpu.VMEM((rows, rank), f32),
-            pltpu.VMEM((CHUNK, rank), f32),
+            pltpu.VMEM((rows, rank), f32),
             pltpu.VMEM((2 * rows, rank), bf16),
             pltpu.VMEM((rows, LANES), f32),
             pltpu.VMEM((8, width), f32),
@@ -603,7 +612,7 @@
             pltpu.VMEM((chips, shard, rank), bf16),
             pltpu.VMEM((chips, shard, rank), bf16),
             pltpu.VMEM((chips + 1, shard, rank), bf16),
-            dma((chunks,)), dma((SLOTS,)), dma((2,)), dma, dma, dma,
+            dma((chunks, groups)), dma((SLOTS, groups)), dma((2,)), dma, dma((groups,)), dma,
             dma((peers,)), dma((3 * chips,)),
             dma((peers,)), dma((peers,)),
             dma((peers,)), dma((peers,)),

time: 836 us -> 326 us (0.39)
  Pallas kernels: 827 us -> 317 us
    pallas_call x2, Pallas kernels: 512 us -> 19.3 us  [reorder(): pl.pallas_call(reorder_kernel, out_shape=tuple((jax.ShapeDtypeStruct(a.sh...]
    pallas_call x1, Pallas kernels: 315 us -> 298 us  [per_device(): pl.pallas_call(functools.partial(relay_kernel, section_count, peers), out...]
where the time goes in v3:
time: 326 us
  Pallas kernels  317 us (97%)
  local copies, waits for them, and re-layouts  6.01 us (2%)
    pallas_call x1, Pallas kernels, per_device(): pl.pallas_call(functools.partial(relay_kernel, section_count, peers), out...  298 us
    pallas_call x2, Pallas kernels, reorder(): pl.pallas_call(reorder_kernel, out_shape=tuple((jax.ShapeDtypeStruct(a.sh...  19.3 us

profile of v3, /device:TPU:0, one launch (start us, length us, event | category | flops | bytes accessed | tf_op | source)
XLA Modules:
  0.0 325.6 jit_solution(6485750714525865281)
XLA Ops:
  0.6 1.1 constant_dynamic-slice_fusion.1
  1.7 0.7 fusion.7.signs
  2.4 1.0 fusion.5.matrix
  3.4 9.5 %shard_map.102 = (bf16[2,128,8192]{2,1,0:T(8,128)(2,1)}, bf16[2,128,8192]{2,1,0:T(8,128)(2,1)}) custom-call(s32[2]{0:T(128)} %order.3, bf16[2,128,8192]{2,1,0:T(8,128)(2,1)} %bitcast.11, bf16[2,128,8192]{2,1,0:T(8,128)(2,1)} %refs_1_.1), custom_call_target="tpu_custom_call" | custom-call | tf_op jit(solution)/shard_map/pallas_call | solution.py:556
  12.9 297.9 %shard_map.103 = (f32[256,8192]{1,0:T(8,128)}, f32[1024,512]{1,0:T(8,128)}, f32[1,1024]{1,0:T(1,128)}, f32[128,8192]{1,0:T(8,128)}) custom-call(bf16[256,8192]{1,0:T(8,128)(2,1)} %bitcast.14, bf16[256,8192]{1,0:T(8,128)(2,1)} %bitcast.15, bf16[1024,512]{1,0:T(8,128)(2,1)} %bitcast.17, f32[1,1024]{1,0:T(1,128)} %gain_in.1, f32[2,8192]{1,0:T(2,128)} %fusion.7.signs, ...), custom_call_target="tpu_custom_call" | custom-call | tf_op jit(solution)/shard_map/pallas_call | solution.py:587
  310.8 0.0 copy-start.1
  310.8 0.0 copy-start.2
  310.8 9.8 %shard_map.104 = f32[2,128,8192]{2,1,0:T(8,128)} custom-call(s32[2]{0:T(128)} %order.3, f32[2,128,8192]{2,1,0:T(8,128)} %bitcast.10), custom_call_target="tpu_custom_call" | custom-call | tf_op jit(solution)/shard_map/pallas_call | solution.py:556
  320.6 0.0 copy-start
  320.6 0.0 copy-done.1
  320.6 1.3 copy.14
  321.9 0.0 copy-done.2
  321.9 0.6 copy.15
  322.5 1.0 copy-done
  323.6 2.0 copy.16
Async XLA Ops:
  310.8 9.8 %copy-start.1 = (f32[1024,512]{1,0:T(8,128)S(1)}, f32[1024,512]{1,0:T(8,128)}, u32[]{:S(2)}) copy-start(f32[1024,512]{1,0:T(8,128)} %get-tuple-element.13) | copy-start | bytes 6291460
  310.8 11.1 %copy-start.2 = (f32[1,1024]{1,0:T(1,128)S(1)}, f32[1,1024]{1,0:T(1,128)}, u32[]{:S(2)}) copy-start(f32[1,1024]{1,0:T(1,128)} %get-tuple-element.24) | copy-start | bytes 12292
  320.6 2.9 copy-start

commit v4 on v3

--- a/solution.py
+++ b/solution.py
@@ -50,11 +50,11 @@
 
 
 def relay_kernel(
-    sections, peers, x, top, weight_in, gain_in, signs, matrix, fb_in,
+    sections, peers, x_in, top, weight_in, gain_in, signs, matrix, fb_in, flag,
     gout, dw, gain_out, fb,
-    weight, gain, inbox, outbox, hidden, stage, pre, grad_act, right, sinv, gacc,
+    x, weight, gain, inbox, outbox, hidden, stage, pre, grad_act, right, sinv, gacc,
     gsum, gparts, own_part, sib_out, sib_in, chain_in,
-    recv_sem, send_sem, out_sem, fb_sem, top_sem, own_sem,
+    recv_sem, send_sem, out_sem, fb_sem, top_sem, own_sem, x_sem,
     w_recv, w_send, g_recv, g_send, s_recv, s_send, b_recv, b_send, c_recv, c_send,
 ):
     sec = lax.axis_index("section")
@@ -83,6 +83,8 @@
 
     own_copy = pltpu.make_async_copy(weight_in, weight.at[span(here, shard)], own_sem)
     own_copy.start()
+    x_copy = pltpu.make_async_copy(x_in, x, x_sem)
+    x_copy.start()
     fb_copy = pltpu.make_async_copy(fb_in, fb, fb_sem)
     fb_copy.start()
     group_wide = GROUP * HB
@@ -154,6 +156,23 @@
     pass_left(here, start)
     pass_sibling(here, start)
 
+    swapped = jnp.broadcast_to(flag[0:1, 0:1], (CHUNK, wide)) == 1
+
+    def exchange(ref, c, cols):
+        here_rows, there_rows = span(c, CHUNK), span(c + chunks // 2, CHUNK)
+        first = ref[here_rows, cols].astype(f32)
+        second = ref[there_rows, cols].astype(f32)
+        ref[here_rows, cols] = jnp.where(swapped, second, first).astype(bf16)
+        ref[there_rows, cols] = jnp.where(swapped, first, second).astype(bf16)
+
+    x_copy.wait()
+
+    @pl.loop(0, chunks // 2)
+    def _(c):
+        @pl.loop(0, width // wide)
+        def _(k):
+            exchange(x, c, span(k, wide))
+
     @pl.loop(0, chunks)
     def _(c):
         rows = span(c, CHUNK)
@@ -194,6 +213,13 @@
         for copy in top_copies:
             copy.wait()
 
+        @pl.loop(0, chunks // 2)
+        def _(c):
+            @pl.loop(0, groups)
+            def _(k):
+                for j in range(group_wide // wide):
+                    exchange(inbox.at[k], c, pl.ds(j * wide, wide))
+
     def accumulate(spot):
         other = spot * 2 + 1 - core
         weight_copy(other, sibling, 2).wait_recv()
@@ -270,19 +296,22 @@
 
         @pl.when(sec < last)
         def _():
-            def decode(k, acc):
-                cols = span(k, group_wide)
+            acc = jnp.zeros((CHUNK, rank), f32)
+            held_low = None
+            for k in range(groups):
+                cols = pl.ds(k * group_wide, group_wide)
                 send(c, slot, k).wait_recv()
                 scales = inbox[k, rows, pl.ds(group_wide, LANES)].astype(f32)
                 scale = jnp.concatenate([scales[:, j:j + 1] for j in range(GROUP)], axis=0)
                 value = dot(stack(inbox[k, rows, pl.ds(0, group_wide)]), matrix[...]) * scale
+                if k > 0:
+                    acc = acc + dot(held_low, weight[pl.ds((k - 1) * group_wide, group_wide), :])
                 value = unstack(value, CHUNK) * signs[1:2, cols]
-                low = value.astype(bf16)
+                held_low = value.astype(bf16)
                 stage[half, :, cols] = value
-                inbox[k, rows, pl.ds(0, group_wide)] = low
-                return acc + dot(low, weight[cols, :])
-
-            grad_act[rows, :] = lax.fori_loop(0, groups, decode, jnp.zeros((CHUNK, rank), f32))
+                inbox[k, rows, pl.ds(0, group_wide)] = held_low
+            acc = acc + dot(held_low, weight[pl.ds((groups - 1) * group_wide, group_wide), :])
+            grad_act[rows, :] = acc
 
         pre_here = pre[rows, :]
         sigma = jax.nn.sigmoid(pre_here)
@@ -292,8 +321,10 @@
         inner = jnp.sum(grad_pre.astype(f32) * pre_here, axis=-1, keepdims=True) / width
         scale_inv = sinv[rows, 0:1]
 
-        def layer_block(cols):
-            grad_hidden = dot(grad_pre, weight[cols, :], 1, 1)
+        def back(k):
+            return dot(grad_pre, weight[pl.ds(k * group_wide, group_wide), :], 1, 1)
+
+        def layer_block(cols, grad_hidden):
             normed = x[rows, cols].astype(f32) * scale_inv
             term = grad_hidden * normed
             total = term[0:8]
@@ -304,10 +335,9 @@
 
         @pl.when(sec == 0)
         def _():
-            @pl.loop(0, groups)
-            def _(k):
-                cols = span(k, group_wide)
-                total, grad_out = layer_block(cols)
+            for k in range(groups):
+                cols = pl.ds(k * group_wide, group_wide)
+                total, grad_out = layer_block(cols, back(k))
                 gacc[:, cols] += total
                 stage[half, :, cols] = grad_out
 
@@ -318,10 +348,12 @@
                 for k in range(groups):
                     send(c - SLOTS, slot, k).wait_send()
 
-            @pl.loop(0, groups)
-            def _(k):
-                cols = span(k, group_wide)
-                total, grad_out = layer_block(cols)
+            following = back(0)
+            for k in range(groups):
+                cols = pl.ds(k * group_wide, group_wide)
+                total, grad_out = layer_block(cols, following)
+                if k + 1 < groups:
+                    following = back(k + 1)
                 value = grad_out + fb[kept, cols]
                 sign = signs[0:1, cols]
                 turned = stack(value * sign)
@@ -541,28 +573,23 @@
             chain_copy(k, 1).wait_send()
 
 
-def reorder_kernel(order, *refs):
-    count = len(refs) // 2
-    for source, target in zip(refs[:count], refs[count:]):
-        target[...] = source[...]
-
-
-def reorder(order, arrays, scatter):
-    micro_count, token_count, width = arrays[0].shape
-    rows = 32
-    straight = pl.BlockSpec((1, rows, width), lambda m, i, order: (m, i, 0))
-    picked = pl.BlockSpec((1, rows, width), lambda m, i, order: (order[m], i, 0))
-    source, target = (straight, picked) if scatter else (picked, straight)
+def reorder_kernel(order, source, target):
+    target[...] = source[...]
+
+
+def reorder(order, array):
+    micro_count, token_count, width = array.shape
+    rows = 16
     return pl.pallas_call(
         reorder_kernel,
-        out_shape=tuple(jax.ShapeDtypeStruct(a.shape, a.dtype) for a in arrays),
+        out_shape=jax.ShapeDtypeStruct(array.shape, array.dtype),
         grid_spec=pltpu.PrefetchScalarGridSpec(
             num_scalar_prefetch=1,
             grid=(micro_count, token_count // rows),
-            in_specs=[source] * len(arrays),
-            out_specs=(target,) * len(arrays),
+            in_specs=[pl.BlockSpec((1, rows, width), lambda m, i, order: (m, i, 0))],
+            out_specs=pl.BlockSpec((1, rows, width), lambda m, i, order: (order[m], i, 0)),
         ),
-    )(order, *arrays)
+    )(order, array)
 
 
 def per_device(
@@ -580,7 +607,8 @@
     above = jnp.minimum(section_here + 1, section_count - 1)
     bits = jnp.stack([rotation_bits[section_here], rotation_bits[above]])
     signs = (1 - 2 * bits).astype(f32)
-    x, top = reorder(batch_order, (section_inputs[0], top_grads), False)
+    assert micro_count == 2
+    flag = jnp.broadcast_to(batch_order[0], (1, LANES))
     vmem = pl.BlockSpec(memory_space=pltpu.VMEM)
     hbm = pl.BlockSpec(memory_space=pl.ANY)
     dma = pltpu.SemaphoreType.DMA
@@ -592,9 +620,10 @@
             jax.ShapeDtypeStruct((1, shard), f32),
             jax.ShapeDtypeStruct((token_count, width), f32),
         ),
-        in_specs=[vmem, hbm, hbm, vmem, vmem, vmem, hbm],
+        in_specs=[hbm, hbm, hbm, vmem, vmem, vmem, hbm, vmem],
         out_specs=(hbm, vmem, vmem, vmem),
         scratch_shapes=[
+            pltpu.VMEM((rows, width), bf16),
             pltpu.VMEM((width, rank), bf16),
             pltpu.VMEM((1, width), f32),
             pltpu.VMEM((groups, rows, GROUP * HB + LANES), bf16),
@@ -612,7 +641,7 @@
             pltpu.VMEM((chips, shard, rank), bf16),
             pltpu.VMEM((chips, shard, rank), bf16),
             pltpu.VMEM((chips + 1, shard, rank), bf16),
-            dma((chunks, groups)), dma((SLOTS, groups)), dma((2,)), dma, dma((groups,)), dma,
+            dma((chunks, groups)), dma((SLOTS, groups)), dma((2,)), dma, dma((groups,)), dma, dma,
             dma((peers,)), dma((3 * chips,)),
             dma((peers,)), dma((peers,)),
             dma((peers,)), dma((peers,)),
@@ -623,10 +652,10 @@
             collective_id=0, has_side_effects=True, vmem_limit_bytes=60 * 1024 * 1024
         ),
     )(
-        x.reshape(rows, width), top.reshape(rows, width), weights[0], norm_gains, signs,
-        hadamard(HB).astype(bf16), feedback[0],
+        section_inputs.reshape(rows, width), top_grads.reshape(rows, width), weights[0],
+        norm_gains, signs, hadamard(HB).astype(bf16), feedback[0], flag,
     )
-    (input_grads,) = reorder(batch_order, (gout.reshape(micro_count, token_count, width),), True)
+    input_grads = reorder(batch_order, gout.reshape(micro_count, token_count, width))
     return (input_grads[None], dw[None], gain_share, fb_out[None])
 
 

time: 326 us -> 321 us (0.985)
  Pallas kernels: 317 us -> 311 us
    pallas_call x2 -> x1, Pallas kernels: 19.3 us -> 12.7 us  [reorder(): pl.pallas_call(reorder_kernel, out_shape=jax.ShapeDtypeStruct(array.shape...]
where the time goes in v4:
time: 321 us
  Pallas kernels  311 us (97%)
  local copies, waits for them, and re-layouts  7.17 us (2%)
    pallas_call x1, Pallas kernels, per_device(): pl.pallas_call(functools.partial(relay_kernel, section_count, peers), out...  299 us
    pallas_call x1, Pallas kernels, reorder(): pl.pallas_call(reorder_kernel, out_shape=jax.ShapeDtypeStruct(array.shape...  12.7 us

profile of v4, /device:TPU:0, one launch (start us, length us, event | category | flops | bytes accessed | tf_op | source)
XLA Modules:
  0.0 320.8 jit_solution(1390207272910659002)
XLA Ops:
  0.6 1.2 broadcast_in_dim.14.flag
  1.8 1.0 constant_dynamic-slice_fusion.1
  2.8 0.7 fusion.7.signs
  3.5 1.0 fusion.5.matrix
  4.5 298.6 %shard_map.102 = (f32[256,8192]{1,0:T(8,128)}, f32[1024,512]{1,0:T(8,128)}, f32[1,1024]{1,0:T(1,128)}, f32[128,8192]{1,0:T(8,128)}) custom-call(bf16[256,8192]{1,0:T(8,128)(2,1)} %bitcast.12, bf16[256,8192]{1,0:T(8,128)(2,1)} %bitcast.13, bf16[1024,512]{1,0:T(8,128)(2,1)} %bitcast.17, f32[1,1024]{1,0:T(1,128)} %gain_in.1, f32[2,8192]{1,0:T(2,128)} %fusion.7.signs, ...), custom_call_target="tpu_custom_call" | custom-call | tf_op jit(solution)/shard_map/pallas_call | solution.py:615
  303.1 0.0 copy-start.1
  303.1 0.0 copy-start.2
  303.1 12.7 %shard_map.103 = f32[2,128,8192]{2,1,0:T(8,128)} custom-call(s32[2]{0:T(128)} %order.1, f32[2,128,8192]{2,1,0:T(8,128)} %bitcast.11), custom_call_target="tpu_custom_call" | custom-call | tf_op jit(solution)/shard_map/pallas_call | solution.py:583
  315.8 0.0 copy-start
  315.8 0.0 copy-done.1
  315.8 1.3 copy.14
  317.2 0.0 copy-done.2
  317.2 0.6 copy.15
  317.7 1.0 copy-done
  318.8 2.0 copy.16
Async XLA Ops:
  303.1 12.7 %copy-start.1 = (f32[1024,512]{1,0:T(8,128)S(1)}, f32[1024,512]{1,0:T(8,128)}, u32[]{:S(2)}) copy-start(f32[1024,512]{1,0:T(8,128)} %get-tuple-element.9) | copy-start | bytes 6291460
  303.1 14.0 %copy-start.2 = (f32[1,1024]{1,0:T(1,128)S(1)}, f32[1,1024]{1,0:T(1,128)}, u32[]{:S(2)}) copy-start(f32[1,1024]{1,0:T(1,128)} %get-tuple-element.20) | copy-start | bytes 12292
  315.8 2.9 copy-start

commit v5 on v4

--- a/solution.py
+++ b/solution.py
@@ -579,7 +579,7 @@
 
 def reorder(order, array):
     micro_count, token_count, width = array.shape
-    rows = 16
+    rows = 64
     return pl.pallas_call(
         reorder_kernel,
         out_shape=jax.ShapeDtypeStruct(array.shape, array.dtype),

time: 321 us -> 316 us (0.984)
  Pallas kernels: 311 us -> 306 us
    pallas_call x1, Pallas kernels: 12.7 us -> 7.93 us  [reorder(): pl.pallas_call(reorder_kernel, out_shape=jax.ShapeDtypeStruct(array.shape...]
where the time goes in v5:
time: 316 us
  Pallas kernels  306 us (97%)
  local copies, waits for them, and re-layouts  7.17 us (2%)
    pallas_call x1, Pallas kernels, per_device(): pl.pallas_call(functools.partial(relay_kernel, section_count, peers), out...  299 us
    pallas_call x1, Pallas kernels, reorder(): pl.pallas_call(reorder_kernel, out_shape=jax.ShapeDtypeStruct(array.shape...  7.93 us

profile of v5, /device:TPU:0, one launch (start us, length us, event | category | flops | bytes accessed | tf_op | source)
XLA Modules:
  0.0 316.0 jit_solution(7706219777559130940)
XLA Ops:
  0.6 1.2 broadcast_in_dim.14.flag
  1.8 1.0 constant_dynamic-slice_fusion.1
  2.8 0.7 fusion.7.signs
  3.5 1.0 fusion.5.matrix
  4.5 298.6 %shard_map.102 = (f32[256,8192]{1,0:T(8,128)}, f32[1024,512]{1,0:T(8,128)}, f32[1,1024]{1,0:T(1,128)}, f32[128,8192]{1,0:T(8,128)}) custom-call(bf16[256,8192]{1,0:T(8,128)(2,1)} %bitcast.12, bf16[256,8192]{1,0:T(8,128)(2,1)} %bitcast.13, bf16[1024,512]{1,0:T(8,128)(2,1)} %bitcast.17, f32[1,1024]{1,0:T(1,128)} %gain_in.1, f32[2,8192]{1,0:T(2,128)} %fusion.7.signs, ...), custom_call_target="tpu_custom_call" | custom-call | tf_op jit(solution)/shard_map/pallas_call | solution.py:615
  303.1 0.0 copy-start.1
  303.1 0.0 copy-start.2
  303.1 7.9 %shard_map.103 = f32[2,128,8192]{2,1,0:T(8,128)} custom-call(s32[2]{0:T(128)} %order.1, f32[2,128,8192]{2,1,0:T(8,128)} %bitcast.11), custom_call_target="tpu_custom_call" | custom-call | tf_op jit(solution)/shard_map/pallas_call | solution.py:583
  311.1 0.0 copy-start
  311.1 0.0 copy-done.1
  311.1 1.3 copy.14
  312.4 0.0 copy-done.2
  312.4 0.6 copy.15
  313.0 1.0 copy-done
  314.0 2.0 copy.16
Async XLA Ops:
  303.1 8.0 %copy-start.1 = (f32[1024,512]{1,0:T(8,128)S(1)}, f32[1024,512]{1,0:T(8,128)}, u32[]{:S(2)}) copy-start(f32[1024,512]{1,0:T(8,128)} %get-tuple-element.9) | copy-start | bytes 6291460
  303.1 9.3 %copy-start.2 = (f32[1,1024]{1,0:T(1,128)S(1)}, f32[1,1024]{1,0:T(1,128)}, u32[]{:S(2)}) copy-start(f32[1,1024]{1,0:T(1,128)} %get-tuple-element.20) | copy-start | bytes 12292
  311.1 2.9 copy-start
